TPU v7x, 32 devices: a whole 2x2x4 slice. The times are simulated.
32 devices in a mesh: row: 4 (over x, core), sector: 8 (over z, y).
Axes of the slice: x: 2, y: 2, z: 4, core: 2. Of those that a mesh axis runs over, the one named last changes fastest.
Arguments:
- state: float32 [6, 256, 128, 128], P(None, 'row', 'sector'), may hold values from -6 to 6
- interp_blocks: float32 [16, 16, 32], replicated, may hold values from -0.1 to 0.8
- rotor_offset: int32 [4, 3], replicated, may hold values from 0 to 127
- axial_speed: float32 [6], replicated, may hold values from 0.3 to 1.5
- row_swirl: float32 [4], P('row'), may hold values from -1.5 to 1.5
- diffusivity: float32 [6], replicated, may hold values from 0.05 to 0.3
- coupling: float32 [6, 6], replicated, may hold values from -1.5 to 1.5
Outputs:
- advanced: float32 [6, 256, 128, 128], P(None, 'row', 'sector')
All inputs are finite; a program needn't handle non-finite values.
Results may differ from a plain program's by a relative error of at most 0.0001.
Values sent between devices are 32-bit elements; how exact they have to be, the bound alone decides.
No kernel may reach another device: no remote copies, remote signals or barrier semaphores. Data moves between devices by JAX's collectives and lax.ppermute only.
A program may use at most 128 MiB of HBM per device.

v0:
```python
import functools

import jax
import jax.numpy as jnp
from jax import lax
from jax.experimental import pallas as pl
from jax.experimental.pallas import tpu as pltpu
from jax.sharding import PartitionSpec as P

time_step = 0.4
highest = lax.Precision.HIGHEST
VMEM = pltpu.VMEM
SMEM = pltpu.SMEM
EXTRA = 4
BLOCK = 8
LOW = 8


def whole(space):
    return pl.BlockSpec(memory_space=space)


def held(shape):
    return pltpu.VMEM(tuple(shape), jnp.float32)


def near(value):
    return pltpu.with_memory_space_constraint(value, pltpu.VMEM)


def params():
    return pltpu.CompilerParams(vmem_limit_bytes=16 * 1024 * 1024)


class Plan:
    def __init__(self, state, sectors):
        self.fields, self.axial, self.cycle, self.radial = state.shape
        self.sectors = sectors
        self.base = self.axial // 4
        self.ghost = (2, self.fields, 2, self.cycle, self.radial)
        self.deep = 8
        self.full = self.cycle * sectors
        self.mine = self.radial // sectors
        self.wide = self.mine + 2 * EXTRA
        self.packed = self.deep * self.cycle


    def ranges(self, kind):
        if kind == "mid":
            return ((self.base, self.axial - self.base),)
        return ((0, self.base), (self.axial - self.base, self.axial))

    def kept(self, kind):
        return self.axial - 2 * self.base if kind == "mid" else 2 * self.base

    def owner(self, plane):
        kind = "mid" if self.base <= plane < self.axial - self.base else "ends"
        return kind, self.place(kind, plane)

    def place(self, kind, plane):
        if kind == "mid":
            return plane - self.base
        return plane if plane < self.axial // 2 else plane - self.axial + 2 * self.base


def pack_kernel(plan, state, below, out, planes, tall, sem):
    copy = pltpu.make_async_copy(state.at[:, plan.axial - plan.deep : plan.axial], planes, sem.at[0])
    copy.start()
    tall[...] = jnp.zeros(tall.shape, jnp.float32)
    copy.wait()
    for side, source in enumerate((planes, below)):
        for field in range(plan.fields):
            flat = source[field].reshape(plan.packed, plan.radial)
            tall[EXTRA : EXTRA + plan.radial, :] = flat.T
            for sector in range(plan.sectors):
                out[sector, side * plan.fields + field] = tall[sector * plan.mine : sector * plan.mine + plan.wide, :]


def pack(plan, state, below):
    return pl.pallas_call(
        functools.partial(pack_kernel, plan),
        in_specs=[whole(pl.ANY), whole(VMEM)],
        out_specs=whole(VMEM),
        out_shape=jax.ShapeDtypeStruct((plan.sectors, 2 * plan.fields, plan.wide, plan.packed), jnp.float32),
        scratch_shapes=[
            held((plan.fields, plan.deep, plan.cycle, plan.radial)),
            held((plan.radial + 2 * EXTRA, plan.packed)),
            pltpu.SemaphoreType.DMA((1,)),
        ],
        cost_estimate=pl.CostEstimate(flops=10000000000, transcendentals=0, bytes_accessed=10000000),
        compiler_params=params(),
        name="pack_zone",
    )(state, below)


def zone_kernel(plan, place, offsets, speed, swirl, next_swirl, diffusion, coupling, weights, got, *refs):
    to_here, to_next, token, base, now, later, spread, matrix, made = refs
    token[...] = jnp.zeros(token.shape, jnp.float32)
    fields, deep, cycle, full, wide = plan.fields, plan.deep, plan.cycle, plan.full, plan.wide
    sections = offsets.shape[0]
    row, sector = place[0], place[1]
    terms = fields + 9
    rows = slice(LOW, LOW + wide)
    lane = lax.broadcasted_iota(jnp.int32, (wide, plan.packed), 1) // cycle
    own_lane = lax.broadcasted_iota(jnp.int32, (plan.mine, plan.packed), 1) // cycle
    at_radius = lax.broadcasted_iota(jnp.int32, (wide, full), 0) + sector * plan.mine - EXTRA
    inside = (at_radius >= 0) & (at_radius < plan.radial)
    block = plan.packed // cycle

    for side, w in enumerate((swirl, next_swirl)):
        for f, (axial, around, d, mix) in enumerate(coefficients(plan, speed, w, diffusion, coupling)):
            for number, factor in enumerate((d, *mix, *axial, *around)):
                spread[side * fields * terms + f * terms + number] = jnp.full((8, full), factor, jnp.float32)

    for buffer in (now, later):
        for side in range(2):
            def clear(field, carry, buffer=buffer, side=side):
                for first, after in ((0, LOW), (LOW + wide, buffer.shape[3])):
                    empty = jnp.zeros((buffer.shape[2], after - first, full), jnp.float32)
                    buffer[side, field, :, first:after, :] = empty
                return carry

            lax.fori_loop(0, fields, clear, 0)

    for side in range(2):
        def spread_out(field, carry, side=side):
            for plane in range(deep):
                parts = []
                for first in range(0, plan.sectors, block):
                    total = jnp.zeros((wide, plan.packed), jnp.float32)
                    for number in range(min(block, plan.sectors - first)):
                        turned = got[first + number, side * fields + field]
                        turn = (number - plane) * cycle % plan.packed
                        if turn:
                            turned = pltpu.roll(turned, turn, 1)
                        total = jnp.where(lane == number, turned, total)
                    parts.append(total)
                value = parts[0] if len(parts) == 1 else jnp.concatenate(parts, axis=1)
                base[side, field, 2 + plane, rows, :] = value
                now[side, field, 2 + plane, rows, :] = value
            return carry

        lax.fori_loop(0, fields, spread_out, 0)

    for section in range(sections):
        offset = offsets[section, jnp.minimum(row, offsets.shape[1] - 1)]
        for side in range(2):
            here = lax.rem(full - offset, full) if side == 0 else offset
            shift, cell = here // cycle, lax.rem(here, cycle)
            for target in range(plan.sectors):
                matrix[target * cycle : (target + 1) * cycle, :] = pltpu.roll(
                    weights[cell], lax.rem(target + shift, plan.sectors) * cycle, 1
                )
            other = 1 - side
            first = 2 if other == 1 else deep
            to = deep + 2 if side == 0 else 0
            pairs = [(field, plane) for field in range(fields) for plane in range(2)]
            values = [now[other, field, first + plane, rows, :] for field, plane in pairs]
            turn = matrix[...]
            together = wide % 8 == 0
            if together:
                values = [jnp.concatenate(values, axis=0)]
            results = [
                lax.dot_general(
                    value, turn, (((1,), (1,)), ((), ())), precision=highest, preferred_element_type=jnp.float32
                )
                for value in values
            ]
            for number, (field, plane) in enumerate(pairs):
                if together:
                    value = results[0][number * wide : (number + 1) * wide]
                else:
                    value = results[number]
                now[side, field, to + plane, rows, :] = value
                made[side, field, 2 * section + plane] = now[side, field, to + plane, LOW + EXTRA : LOW + EXTRA + plan.mine, :]
        if section == sections - 1:
            break
        size = deep - 2 * (section + 1)
        step_size = time_step if section == sections - 2 else 0.5 * time_step
        for side in range(2):
            begin = 2 + (deep - size if side == 0 else 0)

            def advance(number, carry, side=side, begin=begin, now=now, later=later, step_size=step_size):
                plane = begin + number
                for f in range(fields):
                    start = side * fields * terms + f * terms
                    factors = [spread[start + number] for number in range(terms)]
                    for first in range(0, wide, 8):
                        tall = min(8, wide - first)
                        factor = lambda k: factors[k] if tall == 8 else factors[k][:tall]
                        here = slice(LOW + first, LOW + first + tall)
                        center = now[side, f, plane, here, :]
                        total = factor(0) * (
                            now[side, f, plane, LOW + first - 1 : LOW + first - 1 + tall, :]
                            + now[side, f, plane, LOW + first + 1 : LOW + first + 1 + tall, :]
                        )
                        for e in range(fields):
                            total += factor(1 + e) * (center if e == f else now[side, e, plane, here, :])
                        for place_at, by in enumerate((-2, -1, 1, 2)):
                            total += factor(1 + fields + place_at) * now[side, f, plane + by, here, :]
                            total += factor(5 + fields + place_at) * pltpu.roll(center, -by % full, 1)
                        value = base[side, f, plane, here, :] + step_size * total
                        later[side, f, plane, here, :] = jnp.where(inside[first : first + tall], value, 0.0)
                return carry

            lax.fori_loop(0, size, advance, 0)
        now, later = later, now

    has_next = (row < offsets.shape[1]).astype(jnp.float32)
    for side, out in enumerate((to_here, to_next)):
        def hand_out(field, carry, side=side, out=out):
            for target in range(plan.sectors):
                total = jnp.zeros((plan.mine, plan.packed), jnp.float32)
                first = target // block * plan.packed
                for number in range(2 * sections):
                    turned = made[side, field, number, :, first : first + plan.packed]
                    turn = (number - target % block) * cycle % plan.packed
                    if turn:
                        turned = pltpu.roll(turned, turn, 1)
                    total = jnp.where(own_lane == number, turned, total)
                out[target, field] = total * has_next if side == 0 else total
            return carry

        lax.fori_loop(0, fields, hand_out, 0)


def zone(plan, place, offsets, scalars, next_swirl, weights, got):
    speed, swirl, diffusion, coupling = scalars
    buffer = held((2, plan.fields, plan.deep + 4, LOW + plan.wide + 8, plan.full))
    rows = -(-(LOW + plan.wide + 8) // 8) * 8
    need = (3 * 2 * plan.fields * (plan.deep + 4) + 2 * plan.fields * (plan.fields + 9)) * rows * plan.full * 4
    sent = jax.ShapeDtypeStruct((plan.sectors, plan.fields, plan.mine, plan.packed), jnp.float32)
    return pl.pallas_call(
        functools.partial(zone_kernel, plan),
        in_specs=[whole(SMEM)] * 7 + [whole(VMEM)] * 2,
        out_specs=[whole(VMEM)] * 3,
        out_shape=[sent, sent, held((8, plan.radial))],
        scratch_shapes=[
            buffer,
            buffer,
            buffer,
            held((2 * plan.fields * (plan.fields + 9), 8, plan.full)),
            held((plan.full, plan.full)),
            held((2, plan.fields, 2 * offsets.shape[0], plan.mine, plan.full)),
        ],
        cost_estimate=pl.CostEstimate(flops=10000000000, transcendentals=0, bytes_accessed=10000000),
        compiler_params=pltpu.CompilerParams(vmem_limit_bytes=need + 6 * 1024 * 1024),
        name="step_zone",
    )(place, offsets, speed, swirl, next_swirl, diffusion, coupling, weights, got)


def unpack_kernel(plan, got, _, *refs):
    *outs, token, tall = refs
    token[...] = jnp.zeros(token.shape, jnp.float32)
    for side in range(2):
        for field in range(plan.fields):
            for sector in range(plan.sectors):
                tall[sector * plan.mine : (sector + 1) * plan.mine, :] = got[sector, side * plan.fields + field]
            flat = tall[...].T
            for section, out in enumerate(outs):
                for plane in range(2):
                    start = (2 * section + plane) * plan.cycle
                    out[side, field, plane] = flat[start : start + plan.cycle]


def unpack(plan, got, sections, after):
    return pl.pallas_call(
        functools.partial(unpack_kernel, plan),
        in_specs=[whole(VMEM)] * 2,
        out_specs=[whole(VMEM)] * (sections + 1),
        out_shape=[held(plan.ghost)] * sections + [held((8, plan.radial))],
        scratch_shapes=[held((plan.radial, plan.packed))],
        cost_estimate=pl.CostEstimate(flops=10000000000, transcendentals=0, bytes_accessed=10000000),
        compiler_params=params(),
        name="unpack_ghosts",
    )(got, near(after[0]))


def edge_shape(plan, kind):
    return held((plan.fields, plan.kept(kind) // 4, 8, plan.radial))


def first_kernel(plan, ranges, kind, state, _, low_ref, high_ref):
    for first, after in ranges:
        start = plan.place(kind, first) // 4

        def body(tile, carry, first=first, start=start):
            for field in range(plan.fields):
                for step in range(4):
                    plane = first + tile * 4 + step
                    rows = slice(2 * step, 2 * step + 2)
                    low_ref[field, start + tile, rows, :] = state[field, plane, 0:2, :]
                    high_ref[field, start + tile, rows, :] = state[field, plane, plan.cycle - 2 : plan.cycle, :]
            return carry

        lax.fori_loop(0, (after - first) // 4, body, 0)


def first_edges(plan, kind, state, after):
    ranges = plan.ranges(kind)
    return pl.pallas_call(
        functools.partial(first_kernel, plan, ranges, kind),
        in_specs=[whole(VMEM), whole(pl.ANY)],
        out_specs=[whole(VMEM)] * 2,
        out_shape=[edge_shape(plan, kind)] * 2,
        cost_estimate=pl.CostEstimate(flops=10000000000, transcendentals=0, bytes_accessed=10000000),
        compiler_params=params(),
        name=f"first_edges_{kind}",
    )(near(state), after)


def coefficients(plan, speed, swirl, diffusion, coupling):
    twelfth = 1.0 / 12.0
    w = swirl[0]
    table = []
    for f in range(plan.fields):
        v, d = speed[f], diffusion[f]
        axial = ((-v - d) * twelfth, (8.0 * v + 16.0 * d) * twelfth, (16.0 * d - 8.0 * v) * twelfth, (v - d) * twelfth)
        cycle = ((-w - d) * twelfth, (8.0 * w + 16.0 * d) * twelfth, (16.0 * d - 8.0 * w) * twelfth, (w - d) * twelfth)
        mix = [coupling[f, e] - 7.0 * d if e == f else coupling[f, e] for e in range(plan.fields)]
        table.append((axial, cycle, d, mix))
    return table


def stage_kernel(plan, stage, kind, names, speed, swirl, diffusion, coupling, *refs):
    ref = dict(zip(names, refs))
    ranges = plan.ranges(kind)
    cycle, radial, last = plan.cycle, plan.radial, stage == 3
    state, work, spread = ref["state"], ref["work"], ref["spread"]
    terms = plan.fields + 9
    for f, (axial, around, d, mix) in enumerate(coefficients(plan, speed, swirl, diffusion, coupling)):
        for number, factor in enumerate((d, *mix, *axial, *around)):
            spread[f * terms + number] = jnp.full((8, radial), factor, jnp.float32)
    lane = lax.broadcasted_iota(jnp.int32, (8, radial), 1)
    not_first = lane > 0
    not_last = lane < radial - 1

    def cells(plane, level):
        if plane < 0:
            return ref["ghosts"][0, :, plane + 2]
        if plane >= plan.axial:
            return ref["ghosts"][1, :, plane - plan.axial]
        if level == 0:
            return state[:, plane]
        owner, at = plan.owner(plane)
        return ref["cells", level, owner][:, at]

    copies = []
    for number, (low, high) in enumerate(ranges):
        size = high - low
        for plane in range(low - 2, high + 2):
            work[:, plane - low + 2, LOW : LOW + cycle, :] = cells(plane, stage)
        for plane in range(low, high):
            owner, at = plan.owner(plane)
            rows = slice(2 * (at % 4), 2 * (at % 4) + 2)
            work[:, plane - low + 2, LOW - 2 : LOW, :] = ref["low halo", owner][:, at // 4, rows, :]
            work[:, plane - low + 2, LOW + cycle : LOW + cycle + 2, :] = ref["high halo", owner][:, at // 4, rows, :]
            if last:
                ref["earlier"][:, plane - low] = cells(plane, 1) + 2.0 * cells(plane, 2)
        start = plan.place(kind, low)

        def compute(tile, steps, low=low, start=start, number=number):
            for f in range(plan.fields):
                factors = [spread[f * terms + number] for number in range(terms)]
                values = {}
                for step in steps:
                    at = tile * 4 + step - start % 4
                    for row in range(0, cycle, 8):
                        here = slice(LOW + row, LOW + row + 8)
                        center = work[f, at + 2, here, :]
                        left = jnp.where(not_first, pltpu.roll(center, 1, 1), 0.0)
                        right = jnp.where(not_last, pltpu.roll(center, radial - 1, 1), 0.0)
                        total = factors[0] * (left + right)
                        for e in range(plan.fields):
                            total += factors[1 + e] * (center if e == f else work[e, at + 2, here, :])
                        for place, by in enumerate((-2, -1, 1, 2)):
                            total += factors[1 + plan.fields + place] * work[f, at + 2 + by, here, :]
                            beside = slice(LOW + row + by, LOW + row + by + 8)
                            total += factors[5 + plan.fields + place] * work[f, at + 2, beside, :]
                        base = state[f, low + at, row : row + 8, :]
                        if last:
                            value = (ref["earlier"][f, at, row : row + 8, :] + center - base) * (1.0 / 3.0)
                            value += (time_step / 6.0) * total
                        else:
                            value = base + (time_step if stage == 2 else 0.5 * time_step) * total
                        values[step, row] = value
                for (step, row), value in values.items():
                    at = tile * 4 + step - start % 4
                    if last:
                        ref["made"][number, f, at, row : row + 8, :] = value
                        continue
                    ref["out"][f, start + at, row : row + 8, :] = value
                    rows = slice(2 * step, 2 * step + 2)
                    if row == 0:
                        ref["low edge"][f, start // 4 + tile, rows, :] = value[:2]
                    if row == cycle - 8:
                        ref["high edge"][f, start // 4 + tile, rows, :] = value[6:]

        def whole_tile(tile, carry, compute=compute):
            compute(tile, range(4))
            return carry

        block = BLOCK // 4 if last else size // 4
        for first in range(0, size // 4, block):
            after = min(first + block, size // 4)
            lax.fori_loop(first, after, whole_tile, 0)
            if last:
                copies.append(
                    pltpu.make_async_copy(
                        ref["made"].at[number, :, 4 * first : 4 * after],
                        ref["result"].at[:, low + 4 * first : low + 4 * after],
                        ref["sem"].at[len(copies)],
                    )
                )
                copies[-1].start()
    for item in copies:
        item.wait()
    ref["token"][...] = jnp.zeros(ref["token"].shape, jnp.float32)


def stage_call(plan, stage, kind, scalars, state, levels, halos, ghosts, after, result=None):
    ranges = plan.ranges(kind)
    last = stage == 3
    longest = max(high - low for low, high in ranges)
    operands = {"state": near(state)}
    specs = [whole(VMEM)]

    def add(name, value):
        operands[name] = near(value)
        specs.append(whole(VMEM))

    kinds = {plan.owner(plane)[0] for low, high in ranges for plane in range(low, high)}
    for owner in sorted(kinds):
        add(("low halo", owner), halos[owner][0])
        add(("high halo", owner), halos[owner][1])
    for level in (1, 2, stage) if last else (stage,) if stage else ():
        edge = 2 if level == stage else 0
        planes = [plane for low, high in ranges for plane in range(max(0, low - edge), min(plan.axial, high + edge))]
        for owner in sorted({plan.owner(plane)[0] for plane in planes}):
            add(("cells", level, owner), levels[level][owner])
    if kind == "ends":
        add("ghosts", ghosts)
    for number, token in enumerate(after):
        add(("after", number), token)
    aliases = {}
    if result is not None:
        aliases = {len(scalars) + len(operands): 0}
        operands["earlier result"] = result
        specs.append(whole(pl.ANY))
    token = held((8, plan.radial))
    if last:
        outs = {"result": jax.ShapeDtypeStruct(state.shape, jnp.float32), "token": token}
    else:
        edges = edge_shape(plan, kind)
        cells = held((plan.fields, plan.kept(kind), plan.cycle, plan.radial))
        outs = {"out": cells, "low edge": edges, "high edge": edges, "token": token}
    scratch = {
        "work": held((plan.fields, longest + 4, plan.cycle + 16, plan.radial)),
        "spread": held((plan.fields * (plan.fields + 9), 8, plan.radial)),
    }
    if last:
        scratch["earlier"] = held((plan.fields, longest, plan.cycle, plan.radial))
        scratch["made"] = held((len(ranges), plan.fields, longest, plan.cycle, plan.radial))
        scratch["sem"] = pltpu.SemaphoreType.DMA((sum(-(-(high - low) // BLOCK) for low, high in ranges),))
    names = (*operands, *outs, *scratch)
    return pl.pallas_call(
        functools.partial(stage_kernel, plan, stage, kind, names),
        in_specs=[whole(SMEM)] * len(scalars) + specs,
        out_specs=[whole(pl.ANY if name == "result" else VMEM) for name in outs],
        out_shape=list(outs.values()),
        scratch_shapes=list(scratch.values()),
        input_output_aliases=aliases,
        cost_estimate=pl.CostEstimate(flops=10000000000, transcendentals=0, bytes_accessed=10000000),
        compiler_params=params(),
        name=f"stage{stage}_{kind}",
    )(*scalars, *operands.values())


def exchange(edges):
    size = lax.axis_size("sector")
    ahead = [(i, (i + 1) % size) for i in range(size)]
    back = [(i, (i - 1) % size) for i in range(size)]
    low_edges, high_edges = edges
    return lax.ppermute(high_edges, "sector", ahead), lax.ppermute(low_edges, "sector", back)


def on_device(state, interp_blocks, rotor_offset, axial_speed, row_swirl, diffusivity, coupling):
    plan = Plan(state, lax.axis_size("sector"))
    rows = lax.axis_size("row")
    sections = rotor_offset.shape[0]
    place = jnp.stack([lax.axis_index("row"), lax.axis_index("sector")]).astype(jnp.int32)
    scalars = (axial_speed, row_swirl, diffusivity, coupling)
    back = [(row + 1, row) for row in range(rows - 1)]
    ahead = [(row, row + 1) for row in range(rows - 1)]

    below = lax.ppermute(state[:, : plan.deep], "row", back)
    next_swirl = lax.ppermute(row_swirl, "row", back)
    weights = jnp.pad(interp_blocks, ((0, 0), (0, 0), (0, plan.full - interp_blocks.shape[2])))
    packed = pack(plan, state, below)
    levels, halos = [None], [{}]
    got = lax.all_to_all(packed, "sector", 0, 0, tiled=True)
    for kind in ("mid", "ends"):
        halos[0][kind] = exchange(first_edges(plan, kind, state, packed))
    token, result, ghosts = (), None, None

    def step(stage, kind):
        nonlocal token, result
        ghost = ghosts[stage] if kind == "ends" else None
        outs = stage_call(plan, stage, kind, scalars, state, levels, halos[stage], ghost, token, result if stage == sections - 1 else None)
        token = outs[-1:]
        if stage == sections - 1:
            result = outs[0]
            return None
        if len(levels) == stage + 1:
            levels.append({})
            halos.append({})
        levels[stage + 1][kind] = outs[0]
        return outs[1:3]

    def send(stage, kind, edges):
        halos[stage + 1][kind] = exchange(edges)

    def go(stage, kind):
        edges = step(stage, kind)
        if edges is not None:
            send(stage, kind, edges)

    downstream, to_next, *token = zone(plan, place, rotor_offset, scalars, next_swirl, weights, got)
    upstream = lax.ppermute(to_next, "row", ahead)
    mid_edges = step(0, "mid")
    joined = jnp.concatenate([upstream, downstream], axis=1)
    joined, *rest = lax.optimization_barrier((joined, *token, *mid_edges, *halos[0]["ends"]))
    token, mid_edges, halos[0]["ends"] = rest[:1], rest[1:3], rest[3:]
    returned = lax.all_to_all(joined, "sector", 0, 0, tiled=True)
    send(0, "mid", mid_edges)
    *ghosts, last_token = unpack(plan, returned, sections, token)
    token = (last_token,)
    go(0, "ends")
    for stage in range(1, sections):
        go(stage, "mid")
        go(stage, "ends")
    return result


def solution(mesh):
    return jax.shard_map(
        on_device,
        mesh=mesh,
        in_specs=(P(None, "row", "sector", None), P(), P(), P(), P("row"), P(), P()),
        out_specs=P(None, "row", "sector", None),
        check_vma=False,
    )
```

profile of v0, /device:TPU:0, one launch (start us, length us, event | category | flops | bytes accessed | tf_op | source)
XLA Modules:
  0.0 161.7 jit_solution(3896479536330955170)
XLA Ops:
  0.0 1.0 slice.3
  1.0 1.3 collective-permute-start.1
  2.3 2.3 %collective-permute-done.1.below = f32[6,8,16,128]{3,2,1,0:T(8,128)S(1)} collective-permute-done((f32[6,8,16,128]{3,2,1,0:T(8,128)S(1)}, f32[6,8,16,128]{3,2,1,0:T(8,128)S(1)}, u32[]{:S(2)}, u32[]{:S(2)}) %collective-permute-start.1) | collective-permute-done | bytes 393248 | tf_op jit(solution)/shard_map/ppermute | solution.py:496
  4.6 1.9 %copy-done = f32[6,64,16,128]{3,2,1,0:T(8,128)S(1)} copy-done((f32[6,64,16,128]{3,2,1,0:T(8,128)S(1)}, f32[6,64,16,128]{3,2,1,0:T(8,128)}, u32[]{:S(2)}) %copy-start) | copy-done | bytes 3145752
  6.5 1.4 pack_zone.1._
  8.0 0.0 copy-start.10
  8.0 7.4 %all-to-all-start = ((f32[8,12,24,128]{3,2,1,0:T(8,128)}), f32[8,12,24,128]{3,2,1,0:T(8,128)S(1)}, u32[]{:S(2)}, u32[]{:S(2)}) async-start(f32[8,12,24,128]{3,2,1,0:T(8,128)} %pack_zone.1._), calls=%async_computation | async-start | bytes 2359296 | tf_op jit(solution)/shard_map/all_to_all | solution.py:501
  15.4 1.3 collective-permute-start
  17.4 0.1 pad_add_fusion.place
  17.5 1.9 %copy-done.1 = f32[6,64,16,128]{3,2,1,0:T(8,128)S(1)} copy-done((f32[6,64,16,128]{3,2,1,0:T(8,128)S(1)}, f32[6,64,16,128]{3,2,1,0:T(8,128)}, u32[]{:S(2)}) %copy-start.1) | copy-done | bytes 3145752
  19.3 0.2 first_edges_mid.1
  19.5 2.1 %collective-permute-start.3 = (f32[6,8,8,128]{3,2,1,0:T(8,128)S(1)}, f32[6,8,8,128]{3,2,1,0:T(8,128)S(1)}, u32[]{:S(2)}, u32[]{:S(2)}) collective-permute-start(f32[6,8,8,128]{3,2,1,0:T(8,128)S(1)} %get-tuple-element.52), channel_id=1, source_target_pairs={{0,1},{1,2},{2,3},{3,4},{4,5},{5,6},{6,7},{7,0},{8,9},{9,10},{10,1... | collective-permute-start | bytes 589832 | tf_op jit(solution)/shard_map/ppermute | solution.py:484
  21.6 2.8 %collective-permute-start.4 = (f32[6,8,8,128]{3,2,1,0:T(8,128)S(1)}, f32[6,8,8,128]{3,2,1,0:T(8,128)S(1)}, u32[]{:S(2)}, u32[]{:S(2)}) collective-permute-start(f32[6,8,8,128]{3,2,1,0:T(8,128)S(1)} %get-tuple-element.53), channel_id=1, source_target_pairs={{0,7},{1,0},{2,1},{3,2},{4,3},{5,4},{6,5},{7,6},{8,15},{9,8},{10,9... | collective-permute-start | bytes 589832 | tf_op jit(solution)/shard_map/ppermute | solution.py:484
  24.4 0.2 first_edges_ends.1
  24.6 0.1 collective-permute-start.5
  24.7 4.7 %collective-permute-start.6 = (f32[6,8,8,128]{3,2,1,0:T(8,128)S(1)}, f32[6,8,8,128]{3,2,1,0:T(8,128)S(1)}, u32[]{:S(2)}, u32[]{:S(2)}) collective-permute-start(f32[6,8,8,128]{3,2,1,0:T(8,128)S(1)} %get-tuple-element.59), channel_id=1, source_target_pairs={{0,7},{1,0},{2,1},{3,2},{4,3},{5,4},{6,5},{7,6},{8,15},{9,8},{10,9... | collective-permute-start | bytes 589832 | tf_op jit(solution)/shard_map/ppermute | solution.py:484
  29.4 13.1 %all-to-all-done.got = f32[8,12,24,128]{3,2,1,0:T(8,128)S(1)} async-done(((f32[8,12,24,128]{3,2,1,0:T(8,128)}), f32[8,12,24,128]{3,2,1,0:T(8,128)S(1)}, u32[]{:S(2)}, u32[]{:S(2)}) %all-to-all-start) | async-done | bytes 1179680 | tf_op jit(solution)/shard_map/all_to_all | solution.py:501
  42.5 0.0 copy-start.2
  42.5 12.7 %step_zone.1 = (f32[8,6,16,128]{3,2,1,0:T(8,128)S(1)}, f32[8,6,16,128]{3,2,1,0:T(8,128)S(1)}, f32[8,128]{1,0:T(8,128)S(1)}) custom-call(s32[2]{0:T(128)S(1)} %pad_add_fusion.place, s32[4,3]{1,0:T(4,128)S(1)} %copy-done.5, f32[6]{0:T(128)S(1)} %copy-done.6, f32[1]{0:T(128)S(6)} %copy.10.swirl, f32[1]{0:T(128)} %collective-permute-done.next_swirl, ...), custom_call_target="tpu_custom_call" | custom-call | flops 10000000000 | bytes 10000000 | tf_op jit(solution)/shard_map/step_zone/pallas_call | solution.py:233
  55.3 7.7 %collective-permute-start.2 = (f32[8,6,16,128]{3,2,1,0:T(8,128)S(1)}, f32[8,6,16,128]{3,2,1,0:T(8,128)S(1)}, u32[]{:S(2)}, u32[]{:S(2)}) collective-permute-start(f32[8,6,16,128]{3,2,1,0:T(8,128)S(1)} %get-tuple-element.50), channel_id=1, source_target_pairs={{0,8},{8,16},{16,24},{1,9},{9,17},{17,25},{2,10},{10,18},{18,26},{... | collective-permute-start | bytes 1179656 | tf_op jit(solution)/shard_map/ppermute | solution.py:529
  63.0 3.5 %stage0_mid.1 = (f32[6,32,16,128]{3,2,1,0:T(8,128)S(1)}, f32[6,8,8,128]{3,2,1,0:T(8,128)S(1)}, f32[6,8,8,128]{3,2,1,0:T(8,128)S(1)}, f32[8,128]{1,0:T(8,128)S(1)}) custom-call(f32[6]{0:T(128)S(1)} %copy-done.6, f32[1]{0:T(128)S(6)} %copy.10.swirl, f32[6]{0:T(128)S(1)} %copy-done.7, f32[6,6]{1,0:T(8,128)S(1)} %copy-done.4, f32[6,64,16,128]{3,2,1,0:T(8,128)S(1)} %copy-done.2, ...), custom_call_target="tpu_custom_call" | custom-call | flops 10000000000 | bytes 10000000 | tf_op jit(solution)/shard_map/stage0_mid/pallas_call | solution.py:466
  66.6 1.0 pad_maximum_fusion
  67.6 0.3 copy-done.8
  68.0 8.1 %all-to-all-start.1 = ((f32[8,12,16,128]{3,2,1,0:T(8,128)}), f32[8,12,16,128]{3,2,1,0:T(8,128)S(1)}, u32[]{:S(2)}, u32[]{:S(2)}) async-start(f32[8,12,16,128]{3,2,1,0:T(8,128)} %pad_maximum_fusion), calls=%async_computation.1 | async-start | bytes 1572864 | tf_op jit(solution)/shard_map/all_to_all | solution.py:534
  76.0 2.3 %collective-permute-start.9 = (f32[6,8,8,128]{3,2,1,0:T(8,128)S(1)}, f32[6,8,8,128]{3,2,1,0:T(8,128)S(1)}, u32[]{:S(2)}, u32[]{:S(2)}) collective-permute-start(f32[6,8,8,128]{3,2,1,0:T(8,128)S(1)} %get-tuple-element.71), channel_id=1, source_target_pairs={{0,1},{1,2},{2,3},{3,4},{4,5},{5,6},{6,7},{7,0},{8,9},{9,10},{10,1... | collective-permute-start | bytes 589832 | tf_op jit(solution)/shard_map/ppermute | solution.py:484
  78.3 2.5 %collective-permute-start.10 = (f32[6,8,8,128]{3,2,1,0:T(8,128)S(1)}, f32[6,8,8,128]{3,2,1,0:T(8,128)S(1)}, u32[]{:S(2)}, u32[]{:S(2)}) collective-permute-start(f32[6,8,8,128]{3,2,1,0:T(8,128)S(1)} %get-tuple-element.72), channel_id=1, source_target_pairs={{0,7},{1,0},{2,1},{3,2},{4,3},{5,4},{6,5},{7,6},{8,15},{9,8},{10,9... | collective-permute-start | bytes 589832 | tf_op jit(solution)/shard_map/ppermute | solution.py:484
  80.8 16.9 %all-to-all-done.1.got = f32[8,12,16,128]{3,2,1,0:T(8,128)S(1)} async-done(((f32[8,12,16,128]{3,2,1,0:T(8,128)}), f32[8,12,16,128]{3,2,1,0:T(8,128)S(1)}, u32[]{:S(2)}, u32[]{:S(2)}) %all-to-all-start.1) | async-done | bytes 786464 | tf_op jit(solution)/shard_map/all_to_all | solution.py:534
  97.7 0.3 unpack_ghosts.1
  97.9 1.6 %copy-done.3 = f32[6,64,16,128]{3,2,1,0:T(8,128)S(1)} copy-done((f32[6,64,16,128]{3,2,1,0:T(8,128)S(1)}, f32[6,64,16,128]{3,2,1,0:T(8,128)}, u32[]{:S(2)}) %copy-start.3) | copy-done | bytes 3145752
  99.6 3.5 %stage0_ends.1 = (f32[6,32,16,128]{3,2,1,0:T(8,128)S(1)}, f32[6,8,8,128]{3,2,1,0:T(8,128)S(1)}, f32[6,8,8,128]{3,2,1,0:T(8,128)S(1)}, f32[8,128]{1,0:T(8,128)S(1)}) custom-call(f32[6]{0:T(128)S(1)} %copy-done.6, f32[1]{0:T(128)S(6)} %copy.10.swirl, f32[6]{0:T(128)S(1)} %copy-done.7, f32[6,6]{1,0:T(8,128)S(1)} %copy-done.4, f32[6,64,16,128]{3,2,1,0:T(8,128)S(1)} %copy-done.3, ...), custom_call_target="tpu_custom_call" | custom-call | flops 10000000000 | bytes 10000000 | tf_op jit(solution)/shard_map/stage0_ends/pallas_call | solution.py:466
  103.1 5.3 %collective-permute-start.7 = (f32[6,8,8,128]{3,2,1,0:T(8,128)S(1)}, f32[6,8,8,128]{3,2,1,0:T(8,128)S(1)}, u32[]{:S(2)}, u32[]{:S(2)}) collective-permute-start(f32[6,8,8,128]{3,2,1,0:T(8,128)S(1)} %get-tuple-element.66), channel_id=1, source_target_pairs={{0,1},{1,2},{2,3},{3,4},{4,5},{5,6},{6,7},{7,0},{8,9},{9,10},{10,1... | collective-permute-start | bytes 589832 | tf_op jit(solution)/shard_map/ppermute | solution.py:484
  108.4 3.5 %stage1_mid.1 = (f32[6,32,16,128]{3,2,1,0:T(8,128)S(1)}, f32[6,8,8,128]{3,2,1,0:T(8,128)S(1)}, f32[6,8,8,128]{3,2,1,0:T(8,128)S(1)}, f32[8,128]{1,0:T(8,128)S(1)}) custom-call(f32[6]{0:T(128)S(1)} %copy-done.6, f32[1]{0:T(128)S(6)} %copy.10.swirl, f32[6]{0:T(128)S(1)} %copy-done.7, f32[6,6]{1,0:T(8,128)S(1)} %copy-done.4, f32[6,64,16,128]{3,2,1,0:T(8,128)S(1)} %copy-done.3, ...), custom_call_target="tpu_custom_call" | custom-call | flops 10000000000 | bytes 10000000 | tf_op jit(solution)/shard_map/stage1_mid/pallas_call | solution.py:466
  112.0 2.1 %collective-permute-start.13 = (f32[6,8,8,128]{3,2,1,0:T(8,128)S(1)}, f32[6,8,8,128]{3,2,1,0:T(8,128)S(1)}, u32[]{:S(2)}, u32[]{:S(2)}) collective-permute-start(f32[6,8,8,128]{3,2,1,0:T(8,128)S(1)} %get-tuple-element.80), channel_id=1, source_target_pairs={{0,1},{1,2},{2,3},{3,4},{4,5},{5,6},{6,7},{7,0},{8,9},{9,10},{10,1... | collective-permute-start | bytes 589832 | tf_op jit(solution)/shard_map/ppermute | solution.py:484
  114.0 2.7 %collective-permute-start.14 = (f32[6,8,8,128]{3,2,1,0:T(8,128)S(1)}, f32[6,8,8,128]{3,2,1,0:T(8,128)S(1)}, u32[]{:S(2)}, u32[]{:S(2)}) collective-permute-start(f32[6,8,8,128]{3,2,1,0:T(8,128)S(1)} %get-tuple-element.81), channel_id=1, source_target_pairs={{0,7},{1,0},{2,1},{3,2},{4,3},{5,4},{6,5},{7,6},{8,15},{9,8},{10,9... | collective-permute-start | bytes 589832 | tf_op jit(solution)/shard_map/ppermute | solution.py:484
  116.7 5.3 %collective-permute-done.7.refs_1_ = f32[6,8,8,128]{3,2,1,0:T(8,128)S(1)} collective-permute-done((f32[6,8,8,128]{3,2,1,0:T(8,128)S(1)}, f32[6,8,8,128]{3,2,1,0:T(8,128)S(1)}, u32[]{:S(2)}, u32[]{:S(2)}) %collective-permute-start.7) | collective-permute-done | bytes 196640 | tf_op jit(solution)/shard_map/ppermute | solution.py:484
  122.1 3.6 %stage1_ends.1 = (f32[6,32,16,128]{3,2,1,0:T(8,128)S(1)}, f32[6,8,8,128]{3,2,1,0:T(8,128)S(1)}, f32[6,8,8,128]{3,2,1,0:T(8,128)S(1)}, f32[8,128]{1,0:T(8,128)S(1)}) custom-call(f32[6]{0:T(128)S(1)} %copy-done.6, f32[1]{0:T(128)S(6)} %copy.10.swirl, f32[6]{0:T(128)S(1)} %copy-done.7, f32[6,6]{1,0:T(8,128)S(1)} %copy-done.4, f32[6,64,16,128]{3,2,1,0:T(8,128)S(1)} %copy-done.3, ...), custom_call_target="tpu_custom_call" | custom-call | flops 10000000000 | bytes 10000000 | tf_op jit(solution)/shard_map/stage1_ends/pallas_call | solution.py:466
  125.6 2.5 %collective-permute-start.11 = (f32[6,8,8,128]{3,2,1,0:T(8,128)S(1)}, f32[6,8,8,128]{3,2,1,0:T(8,128)S(1)}, u32[]{:S(2)}, u32[]{:S(2)}) collective-permute-start(f32[6,8,8,128]{3,2,1,0:T(8,128)S(1)} %get-tuple-element.75), channel_id=1, source_target_pairs={{0,1},{1,2},{2,3},{3,4},{4,5},{5,6},{6,7},{7,0},{8,9},{9,10},{10,1... | collective-permute-start | bytes 589832 | tf_op jit(solution)/shard_map/ppermute | solution.py:484
  128.2 2.2 %collective-permute-start.12 = (f32[6,8,8,128]{3,2,1,0:T(8,128)S(1)}, f32[6,8,8,128]{3,2,1,0:T(8,128)S(1)}, u32[]{:S(2)}, u32[]{:S(2)}) collective-permute-start(f32[6,8,8,128]{3,2,1,0:T(8,128)S(1)} %get-tuple-element.76), channel_id=1, source_target_pairs={{0,7},{1,0},{2,1},{3,2},{4,3},{5,4},{6,5},{7,6},{8,15},{9,8},{10,9... | collective-permute-start | bytes 589832 | tf_op jit(solution)/shard_map/ppermute | solution.py:484
  130.4 3.6 %stage2_mid.1 = (f32[6,32,16,128]{3,2,1,0:T(8,128)S(1)}, f32[6,8,8,128]{3,2,1,0:T(8,128)S(1)}, f32[6,8,8,128]{3,2,1,0:T(8,128)S(1)}, f32[8,128]{1,0:T(8,128)S(1)}) custom-call(f32[6]{0:T(128)S(1)} %copy-done.6, f32[1]{0:T(128)S(6)} %copy.10.swirl, f32[6]{0:T(128)S(1)} %copy-done.7, f32[6,6]{1,0:T(8,128)S(1)} %copy-done.4, f32[6,64,16,128]{3,2,1,0:T(8,128)S(1)} %copy-done.3, ...), custom_call_target="tpu_custom_call" | custom-call | flops 10000000000 | bytes 10000000 | tf_op jit(solution)/shard_map/stage2_mid/pallas_call | solution.py:466
  134.0 0.1 collective-permute-start.17
  134.0 4.7 %collective-permute-start.18 = (f32[6,8,8,128]{3,2,1,0:T(8,128)S(1)}, f32[6,8,8,128]{3,2,1,0:T(8,128)S(1)}, u32[]{:S(2)}, u32[]{:S(2)}) collective-permute-start(f32[6,8,8,128]{3,2,1,0:T(8,128)S(1)} %get-tuple-element.90), channel_id=1, source_target_pairs={{0,7},{1,0},{2,1},{3,2},{4,3},{5,4},{6,5},{7,6},{8,15},{9,8},{10,9... | collective-permute-start | bytes 589832 | tf_op jit(solution)/shard_map/ppermute | solution.py:484
  138.8 1.8 %collective-permute-done.11.refs_1_ = f32[6,8,8,128]{3,2,1,0:T(8,128)S(1)} collective-permute-done((f32[6,8,8,128]{3,2,1,0:T(8,128)S(1)}, f32[6,8,8,128]{3,2,1,0:T(8,128)S(1)}, u32[]{:S(2)}, u32[]{:S(2)}) %collective-permute-start.11) | collective-permute-done | bytes 196640 | tf_op jit(solution)/shard_map/ppermute | solution.py:484
  140.6 2.5 %collective-permute-done.12.refs_2_ = f32[6,8,8,128]{3,2,1,0:T(8,128)S(1)} collective-permute-done((f32[6,8,8,128]{3,2,1,0:T(8,128)S(1)}, f32[6,8,8,128]{3,2,1,0:T(8,128)S(1)}, u32[]{:S(2)}, u32[]{:S(2)}) %collective-permute-start.12) | collective-permute-done | bytes 196640 | tf_op jit(solution)/shard_map/ppermute | solution.py:484
  143.1 3.5 %stage2_ends.1 = (f32[6,32,16,128]{3,2,1,0:T(8,128)S(1)}, f32[6,8,8,128]{3,2,1,0:T(8,128)S(1)}, f32[6,8,8,128]{3,2,1,0:T(8,128)S(1)}, f32[8,128]{1,0:T(8,128)S(1)}) custom-call(f32[6]{0:T(128)S(1)} %copy-done.6, f32[1]{0:T(128)S(6)} %copy.10.swirl, f32[6]{0:T(128)S(1)} %copy-done.7, f32[6,6]{1,0:T(8,128)S(1)} %copy-done.4, f32[6,64,16,128]{3,2,1,0:T(8,128)S(1)} %copy-done.3, ...), custom_call_target="tpu_custom_call" | custom-call | flops 10000000000 | bytes 10000000 | tf_op jit(solution)/shard_map/stage2_ends/pallas_call | solution.py:466
  146.7 0.1 collective-permute-start.15
  146.7 4.7 %collective-permute-start.16 = (f32[6,8,8,128]{3,2,1,0:T(8,128)S(1)}, f32[6,8,8,128]{3,2,1,0:T(8,128)S(1)}, u32[]{:S(2)}, u32[]{:S(2)}) collective-permute-start(f32[6,8,8,128]{3,2,1,0:T(8,128)S(1)} %get-tuple-element.85), channel_id=1, source_target_pairs={{0,7},{1,0},{2,1},{3,2},{4,3},{5,4},{6,5},{7,6},{8,15},{9,8},{10,9... | collective-permute-start | bytes 589832 | tf_op jit(solution)/shard_map/ppermute | solution.py:484
  151.5 4.8 %stage3_mid.1 = (f32[6,64,16,128]{3,2,1,0:T(8,128)}, f32[8,128]{1,0:T(8,128)S(1)}) custom-call(f32[6]{0:T(128)S(1)} %copy-done.6, f32[1]{0:T(128)S(6)} %copy.10.swirl, f32[6]{0:T(128)S(1)} %copy-done.7, f32[6,6]{1,0:T(8,128)S(1)} %copy-done.4, f32[6,64,16,128]{3,2,1,0:T(8,128)S(1)} %copy-done.3, f32[6,8,8,128]{3,2,1,0:T(8,128)S(1)} %collective-permute-done.17.refs_1_, ...), custom_call_target="tpu_custom_call" | custom-call | flops 10000000000 | bytes 10000000 | tf_op jit(solution)/shard_map/stage3_mid/pallas_call | solution.py:466
  156.2 5.3 %stage3_ends.1 = (f32[6,64,16,128]{3,2,1,0:T(8,128)}, f32[8,128]{1,0:T(8,128)}) custom-call(f32[6]{0:T(128)S(1)} %copy-done.6, f32[1]{0:T(128)S(6)} %copy.10.swirl, f32[6]{0:T(128)S(1)} %copy-done.7, f32[6,6]{1,0:T(8,128)S(1)} %copy-done.4, f32[6,64,16,128]{3,2,1,0:T(8,128)S(1)} %copy-done.3, ...), custom_call_target="tpu_custom_call", output_to_operand_aliasing={{0}: (13, {})} | custom-call | flops 10000000000 | bytes 10000000 | tf_op jit(solution)/shard_map/stage3_ends/pallas_call | solution.py:466
  (33 shorter events, 0.1 us)
Async XLA Ops:
  1.0 3.6 %collective-permute-start.1 = (f32[6,8,16,128]{3,2,1,0:T(8,128)S(1)}, f32[6,8,16,128]{3,2,1,0:T(8,128)S(1)}, u32[]{:S(2)}, u32[]{:S(2)}) collective-permute-start(f32[6,8,16,128]{3,2,1,0:T(8,128)S(1)} %slice.3), channel_id=1, source_target_pairs={{8,0},{16,8},{24,16},{9,1},{17,9},{25,17},{10,2},{18,10},{26,18},{... | collective-permute-start | bytes 1179656 | tf_op jit(solution)/shard_map/ppermute | solution.py:496
  4.6 1.9 %copy-start = (f32[6,64,16,128]{3,2,1,0:T(8,128)S(1)}, f32[6,64,16,128]{3,2,1,0:T(8,128)}, u32[]{:S(2)}) copy-start(f32[6,64,16,128]{3,2,1,0:T(8,128)} %refs_0_.15) | copy-start | bytes 9437188
  8.0 9.4 %copy-start.10 = (f32[16,16,32]{2,1,0:T(8,128)S(1)}, f32[16,16,32]{2,1,0:T(8,128)}, u32[]{:S(2)}) copy-start(f32[16,16,32]{2,1,0:T(8,128)} %param.8) | copy-start | bytes 98308
  8.0 34.5 %all-to-all-start = ((f32[8,12,24,128]{3,2,1,0:T(8,128)}), f32[8,12,24,128]{3,2,1,0:T(8,128)S(1)}, u32[]{:S(2)}, u32[]{:S(2)}) async-start(f32[8,12,24,128]{3,2,1,0:T(8,128)} %pack_zone.1._), calls=%async_computation | async-start | bytes 2359296 | tf_op jit(solution)/shard_map/all_to_all | solution.py:501
  15.4 14.0 %collective-permute-start = (f32[1]{0:T(128)}, f32[1]{0:T(128)}, u32[]{:S(2)}, u32[]{:S(2)}) collective-permute-start(f32[1]{0:T(128)} %param.11), channel_id=1, source_target_pairs={{8,0},{16,8},{24,16},{9,1},{17,9},{25,17},{10,2},{18,10},{26,18},{... | collective-permute-start | bytes 20 | tf_op jit(solution)/shard_map/ppermute | solution.py:497
  17.5 1.9 %copy-start.1 = (f32[6,64,16,128]{3,2,1,0:T(8,128)S(1)}, f32[6,64,16,128]{3,2,1,0:T(8,128)}, u32[]{:S(2)}) copy-start(f32[6,64,16,128]{3,2,1,0:T(8,128)} %refs_0_.15) | copy-start | bytes 9437188
  19.5 43.4 %collective-permute-start.3 = (f32[6,8,8,128]{3,2,1,0:T(8,128)S(1)}, f32[6,8,8,128]{3,2,1,0:T(8,128)S(1)}, u32[]{:S(2)}, u32[]{:S(2)}) collective-permute-start(f32[6,8,8,128]{3,2,1,0:T(8,128)S(1)} %get-tuple-element.52), channel_id=1, source_target_pairs={{0,1},{1,2},{2,3},{3,4},{4,5},{5,6},{6,7},{7,0},{8,9},{9,10},{10,1... | collective-permute-start | bytes 589832 | tf_op jit(solution)/shard_map/ppermute | solution.py:484
  21.6 20.9 %copy-start.4 = (f32[6,6]{1,0:T(8,128)S(1)}, f32[6,6]{1,0:T(8,128)}, u32[]{:S(2)}) copy-start(f32[6,6]{1,0:T(8,128)} %coupling.17) | copy-start | bytes 436
  21.6 20.9 %copy-start.5 = (s32[4,3]{1,0:T(4,128)S(1)}, s32[4,3]{1,0:T(4,128)}, u32[]{:S(2)}) copy-start(s32[4,3]{1,0:T(4,128)} %offsets.1) | copy-start | bytes 148
  21.6 20.9 %copy-start.6 = (f32[6]{0:T(128)S(1)}, f32[6]{0:T(128)}, u32[]{:S(2)}) copy-start(f32[6]{0:T(128)} %speed.17) | copy-start | bytes 76
  21.6 20.9 %copy-start.7 = (f32[6]{0:T(128)S(1)}, f32[6]{0:T(128)}, u32[]{:S(2)}) copy-start(f32[6]{0:T(128)} %diffusion.17) | copy-start | bytes 76
  21.6 41.4 %collective-permute-start.4 = (f32[6,8,8,128]{3,2,1,0:T(8,128)S(1)}, f32[6,8,8,128]{3,2,1,0:T(8,128)S(1)}, u32[]{:S(2)}, u32[]{:S(2)}) collective-permute-start(f32[6,8,8,128]{3,2,1,0:T(8,128)S(1)} %get-tuple-element.53), channel_id=1, source_target_pairs={{0,7},{1,0},{2,1},{3,2},{4,3},{5,4},{6,5},{7,6},{8,15},{9,8},{10,9... | collective-permute-start | bytes 589832 | tf_op jit(solution)/shard_map/ppermute | solution.py:484
  24.6 43.0 %collective-permute-start.5 = (f32[6,8,8,128]{3,2,1,0:T(8,128)S(1)}, f32[6,8,8,128]{3,2,1,0:T(8,128)S(1)}, u32[]{:S(2)}, u32[]{:S(2)}) collective-permute-start(f32[6,8,8,128]{3,2,1,0:T(8,128)S(1)} %get-tuple-element.58), channel_id=1, source_target_pairs={{0,1},{1,2},{2,3},{3,4},{4,5},{5,6},{6,7},{7,0},{8,9},{9,10},{10,1... | collective-permute-start | bytes 589832 | tf_op jit(solution)/shard_map/ppermute | solution.py:484
  24.7 42.9 %collective-permute-start.6 = (f32[6,8,8,128]{3,2,1,0:T(8,128)S(1)}, f32[6,8,8,128]{3,2,1,0:T(8,128)S(1)}, u32[]{:S(2)}, u32[]{:S(2)}) collective-permute-start(f32[6,8,8,128]{3,2,1,0:T(8,128)S(1)} %get-tuple-element.59), channel_id=1, source_target_pairs={{0,7},{1,0},{2,1},{3,2},{4,3},{5,4},{6,5},{7,6},{8,15},{9,8},{10,9... | collective-permute-start | bytes 589832 | tf_op jit(solution)/shard_map/ppermute | solution.py:484
  42.5 20.5 %copy-start.2 = (f32[6,64,16,128]{3,2,1,0:T(8,128)S(1)}, f32[6,64,16,128]{3,2,1,0:T(8,128)}, u32[]{:S(2)}) copy-start(f32[6,64,16,128]{3,2,1,0:T(8,128)} %refs_0_.15) | copy-start | bytes 9437188
  55.3 11.3 %collective-permute-start.2 = (f32[8,6,16,128]{3,2,1,0:T(8,128)S(1)}, f32[8,6,16,128]{3,2,1,0:T(8,128)S(1)}, u32[]{:S(2)}, u32[]{:S(2)}) collective-permute-start(f32[8,6,16,128]{3,2,1,0:T(8,128)S(1)} %get-tuple-element.50), channel_id=1, source_target_pairs={{0,8},{8,16},{16,24},{1,9},{9,17},{17,25},{2,10},{10,18},{18,26},{... | collective-permute-start | bytes 1179656 | tf_op jit(solution)/shard_map/ppermute | solution.py:529
  66.5 1.4 copy-start.8
  68.0 29.7 %all-to-all-start.1 = ((f32[8,12,16,128]{3,2,1,0:T(8,128)}), f32[8,12,16,128]{3,2,1,0:T(8,128)S(1)}, u32[]{:S(2)}, u32[]{:S(2)}) async-start(f32[8,12,16,128]{3,2,1,0:T(8,128)} %pad_maximum_fusion), calls=%async_computation.1 | async-start | bytes 1572864 | tf_op jit(solution)/shard_map/all_to_all | solution.py:534
  76.0 32.4 %collective-permute-start.9 = (f32[6,8,8,128]{3,2,1,0:T(8,128)S(1)}, f32[6,8,8,128]{3,2,1,0:T(8,128)S(1)}, u32[]{:S(2)}, u32[]{:S(2)}) collective-permute-start(f32[6,8,8,128]{3,2,1,0:T(8,128)S(1)} %get-tuple-element.71), channel_id=1, source_target_pairs={{0,1},{1,2},{2,3},{3,4},{4,5},{5,6},{6,7},{7,0},{8,9},{9,10},{10,1... | collective-permute-start | bytes 589832 | tf_op jit(solution)/shard_map/ppermute | solution.py:484
  78.3 30.1 %collective-permute-start.10 = (f32[6,8,8,128]{3,2,1,0:T(8,128)S(1)}, f32[6,8,8,128]{3,2,1,0:T(8,128)S(1)}, u32[]{:S(2)}, u32[]{:S(2)}) collective-permute-start(f32[6,8,8,128]{3,2,1,0:T(8,128)S(1)} %get-tuple-element.72), channel_id=1, source_target_pairs={{0,7},{1,0},{2,1},{3,2},{4,3},{5,4},{6,5},{7,6},{8,15},{9,8},{10,9... | collective-permute-start | bytes 589832 | tf_op jit(solution)/shard_map/ppermute | solution.py:484
  97.7 1.9 %copy-start.3 = (f32[6,64,16,128]{3,2,1,0:T(8,128)S(1)}, f32[6,64,16,128]{3,2,1,0:T(8,128)}, u32[]{:S(2)}) copy-start(f32[6,64,16,128]{3,2,1,0:T(8,128)} %refs_0_.15) | copy-start | bytes 9437188
  99.6 8.8 %copy-start.9 = (f32[6,32,16,128]{3,2,1,0:T(8,128)S(1)}, f32[6,32,16,128]{3,2,1,0:T(8,128)}, u32[]{:S(2)}) copy-start(f32[6,32,16,128]{3,2,1,0:T(8,128)} %copy-done.8) | copy-start | bytes 4718596
  103.1 19.0 %collective-permute-start.7 = (f32[6,8,8,128]{3,2,1,0:T(8,128)S(1)}, f32[6,8,8,128]{3,2,1,0:T(8,128)S(1)}, u32[]{:S(2)}, u32[]{:S(2)}) collective-permute-start(f32[6,8,8,128]{3,2,1,0:T(8,128)S(1)} %get-tuple-element.66), channel_id=1, source_target_pairs={{0,1},{1,2},{2,3},{3,4},{4,5},{5,6},{6,7},{7,0},{8,9},{9,10},{10,1... | collective-permute-start | bytes 589832 | tf_op jit(solution)/shard_map/ppermute | solution.py:484
  108.4 13.7 %collective-permute-start.8 = (f32[6,8,8,128]{3,2,1,0:T(8,128)S(1)}, f32[6,8,8,128]{3,2,1,0:T(8,128)S(1)}, u32[]{:S(2)}, u32[]{:S(2)}) collective-permute-start(f32[6,8,8,128]{3,2,1,0:T(8,128)S(1)} %get-tuple-element.67), channel_id=1, source_target_pairs={{0,7},{1,0},{2,1},{3,2},{4,3},{5,4},{6,5},{7,6},{8,15},{9,8},{10,9... | collective-permute-start | bytes 589832 | tf_op jit(solution)/shard_map/ppermute | solution.py:484
  112.0 18.5 %collective-permute-start.13 = (f32[6,8,8,128]{3,2,1,0:T(8,128)S(1)}, f32[6,8,8,128]{3,2,1,0:T(8,128)S(1)}, u32[]{:S(2)}, u32[]{:S(2)}) collective-permute-start(f32[6,8,8,128]{3,2,1,0:T(8,128)S(1)} %get-tuple-element.80), channel_id=1, source_target_pairs={{0,1},{1,2},{2,3},{3,4},{4,5},{5,6},{6,7},{7,0},{8,9},{9,10},{10,1... | collective-permute-start | bytes 589832 | tf_op jit(solution)/shard_map/ppermute | solution.py:484
  114.0 16.4 %collective-permute-start.14 = (f32[6,8,8,128]{3,2,1,0:T(8,128)S(1)}, f32[6,8,8,128]{3,2,1,0:T(8,128)S(1)}, u32[]{:S(2)}, u32[]{:S(2)}) collective-permute-start(f32[6,8,8,128]{3,2,1,0:T(8,128)S(1)} %get-tuple-element.81), channel_id=1, source_target_pairs={{0,7},{1,0},{2,1},{3,2},{4,3},{5,4},{6,5},{7,6},{8,15},{9,8},{10,9... | collective-permute-start | bytes 589832 | tf_op jit(solution)/shard_map/ppermute | solution.py:484
  125.6 14.9 %collective-permute-start.11 = (f32[6,8,8,128]{3,2,1,0:T(8,128)S(1)}, f32[6,8,8,128]{3,2,1,0:T(8,128)S(1)}, u32[]{:S(2)}, u32[]{:S(2)}) collective-permute-start(f32[6,8,8,128]{3,2,1,0:T(8,128)S(1)} %get-tuple-element.75), channel_id=1, source_target_pairs={{0,1},{1,2},{2,3},{3,4},{4,5},{5,6},{6,7},{7,0},{8,9},{9,10},{10,1... | collective-permute-start | bytes 589832 | tf_op jit(solution)/shard_map/ppermute | solution.py:484
  128.2 14.9 %collective-permute-start.12 = (f32[6,8,8,128]{3,2,1,0:T(8,128)S(1)}, f32[6,8,8,128]{3,2,1,0:T(8,128)S(1)}, u32[]{:S(2)}, u32[]{:S(2)}) collective-permute-start(f32[6,8,8,128]{3,2,1,0:T(8,128)S(1)} %get-tuple-element.76), channel_id=1, source_target_pairs={{0,7},{1,0},{2,1},{3,2},{4,3},{5,4},{6,5},{7,6},{8,15},{9,8},{10,9... | collective-permute-start | bytes 589832 | tf_op jit(solution)/shard_map/ppermute | solution.py:484
  134.0 17.5 %collective-permute-start.17 = (f32[6,8,8,128]{3,2,1,0:T(8,128)S(1)}, f32[6,8,8,128]{3,2,1,0:T(8,128)S(1)}, u32[]{:S(2)}, u32[]{:S(2)}) collective-permute-start(f32[6,8,8,128]{3,2,1,0:T(8,128)S(1)} %get-tuple-element.89), channel_id=1, source_target_pairs={{0,1},{1,2},{2,3},{3,4},{4,5},{5,6},{6,7},{7,0},{8,9},{9,10},{10,1... | collective-permute-start | bytes 589832 | tf_op jit(solution)/shard_map/ppermute | solution.py:484
  134.0 17.4 %collective-permute-start.18 = (f32[6,8,8,128]{3,2,1,0:T(8,128)S(1)}, f32[6,8,8,128]{3,2,1,0:T(8,128)S(1)}, u32[]{:S(2)}, u32[]{:S(2)}) collective-permute-start(f32[6,8,8,128]{3,2,1,0:T(8,128)S(1)} %get-tuple-element.90), channel_id=1, source_target_pairs={{0,7},{1,0},{2,1},{3,2},{4,3},{5,4},{6,5},{7,6},{8,15},{9,8},{10,9... | collective-permute-start | bytes 589832 | tf_op jit(solution)/shard_map/ppermute | solution.py:484
  146.7 9.5 %collective-permute-start.15 = (f32[6,8,8,128]{3,2,1,0:T(8,128)S(1)}, f32[6,8,8,128]{3,2,1,0:T(8,128)S(1)}, u32[]{:S(2)}, u32[]{:S(2)}) collective-permute-start(f32[6,8,8,128]{3,2,1,0:T(8,128)S(1)} %get-tuple-element.84), channel_id=1, source_target_pairs={{0,1},{1,2},{2,3},{3,4},{4,5},{5,6},{6,7},{7,0},{8,9},{9,10},{10,1... | collective-permute-start | bytes 589832 | tf_op jit(solution)/shard_map/ppermute | solution.py:484
  146.7 9.5 %collective-permute-start.16 = (f32[6,8,8,128]{3,2,1,0:T(8,128)S(1)}, f32[6,8,8,128]{3,2,1,0:T(8,128)S(1)}, u32[]{:S(2)}, u32[]{:S(2)}) collective-permute-start(f32[6,8,8,128]{3,2,1,0:T(8,128)S(1)} %get-tuple-element.85), channel_id=1, source_target_pairs={{0,7},{1,0},{2,1},{3,2},{4,3},{5,4},{6,5},{7,6},{8,15},{9,8},{10,9... | collective-permute-start | bytes 589832 | tf_op jit(solution)/shard_map/ppermute | solution.py:484
where the time goes:
time: 162 us
  starting transfers between devices  64.5 us (40%)
  Pallas kernels  46.1 us (28%)
  waiting for transfers between devices  42.1 us (26%)
  local copies, waits for them, and re-layouts  6.82 us (4%)
    pallas_call x8, Pallas kernels, stage_call(): pl.pallas_call(functools.partial(stage_kernel, plan, stage, kind, names),...  31.4 us
    ppermute x8, starting transfers between devices, exchange(): lax.ppermute(low_edges, 'sector', back)  24.4 us
    all_to_all x1, waiting for transfers between devices, on_device(): returned = lax.all_to_all(joined, 'sector', 0, 0, tiled=True)  16.9 us
    ppermute x8, starting transfers between devices, exchange(): lax.ppermute(high_edges, 'sector', ahead)  14.4 us
    all_to_all x1, waiting for transfers between devices, on_device(): got = lax.all_to_all(packed, 'sector', 0, 0, tiled=True)  13.1 us
    pallas_call x1, Pallas kernels, zone(): pl.pallas_call(functools.partial(zone_kernel, plan), in_specs=[whole(SMEM...  12.7 us
    all_to_all x1, starting transfers between devices, on_device(): returned = lax.all_to_all(joined, 'sector', 0, 0, tiled=True)  8.08 us
    ppermute x1, starting transfers between devices, on_device(): upstream = lax.ppermute(to_next, 'row', ahead)  7.69 us
  transfers between devices with their start and end apart: 21, of which 6 were waited for; matrix products, arithmetic and copies ran while one was open for 1% of the time, Pallas kernels for 24%

commit v1 on v0

--- a/solution.py
+++ b/solution.py
@@ -529,8 +529,8 @@
     upstream = lax.ppermute(to_next, "row", ahead)
     mid_edges = step(0, "mid")
     joined = jnp.concatenate([upstream, downstream], axis=1)
-    joined, *rest = lax.optimization_barrier((joined, *token, *mid_edges, *halos[0]["ends"]))
-    token, mid_edges, halos[0]["ends"] = rest[:1], rest[1:3], rest[3:]
+    joined, *rest = lax.optimization_barrier((joined, *token, *mid_edges))
+    token, mid_edges = rest[:1], rest[1:]
     returned = lax.all_to_all(joined, "sector", 0, 0, tiled=True)
     send(0, "mid", mid_edges)
     *ghosts, last_token = unpack(plan, returned, sections, token)

time: 162 us -> 160 us (0.988)
    all_to_all x1, waiting for transfers between devices: 16.9 us -> 10.1 us  [on_device(): returned = lax.all_to_all(joined, 'sector', 0, 0, tiled=True)]
    ppermute x8, starting transfers between devices: 14.4 us -> 20.9 us  [exchange(): lax.ppermute(high_edges, 'sector', ahead)]
    all_to_all x1, waiting for transfers between devices: 13.1 us -> 18.9 us  [on_device(): got = lax.all_to_all(packed, 'sector', 0, 0, tiled=True)]
    all_to_all x1, starting transfers between devices: 8.08 us -> 4.32 us  [on_device(): returned = lax.all_to_all(joined, 'sector', 0, 0, tiled=True)]
    ppermute x8, starting transfers between devices: 24.4 us -> 22 us  [exchange(): lax.ppermute(low_edges, 'sector', back)]
    ppermute x8, waiting for transfers between devices: 2.55 us -> 0.78 us  [exchange(): lax.ppermute(low_edges, 'sector', back)]
    unnamed x22 -> x24, local copies, waits for them, and re-layouts: 5.79 us -> 6.33 us
  transfers between devices with their start and end apart: 21 -> 21, of which waited for: 6 -> 7; matrix products, arithmetic and copies ran while one was open for 1% -> 0% of each run, Pallas kernels for 24% -> 25%
where the time goes in v1:
time: 160 us
  starting transfers between devices  63.6 us (40%)
  Pallas kernels  46.1 us (29%)
  waiting for transfers between devices  40.6 us (25%)
  local copies, waits for them, and re-layouts  7.37 us (5%)
    pallas_call x8, Pallas kernels, stage_call(): pl.pallas_call(functools.partial(stage_kernel, plan, stage, kind, names),...  31.4 us
    ppermute x8, starting transfers between devices, exchange(): lax.ppermute(low_edges, 'sector', back)  22 us
    ppermute x8, starting transfers between devices, exchange(): lax.ppermute(high_edges, 'sector', ahead)  20.9 us
    all_to_all x1, waiting for transfers between devices, on_device(): got = lax.all_to_all(packed, 'sector', 0, 0, tiled=True)  18.9 us
    pallas_call x1, Pallas kernels, zone(): pl.pallas_call(functools.partial(zone_kernel, plan), in_specs=[whole(SMEM...  12.7 us
    all_to_all x1, waiting for transfers between devices, on_device(): returned = lax.all_to_all(joined, 'sector', 0, 0, tiled=True)  10.1 us
    ppermute x8, waiting for transfers between devices, exchange(): lax.ppermute(high_edges, 'sector', ahead)  8.44 us
    all_to_all x1, starting transfers between devices, on_device(): got = lax.all_to_all(packed, 'sector', 0, 0, tiled=True)  7.42 us
  transfers between devices with their start and end apart: 21, of which 7 were waited for; matrix products, arithmetic and copies ran while one was open for 0% of the time, Pallas kernels for 25%

profile of v1, /device:TPU:0, one launch (start us, length us, event | category | flops | bytes accessed | tf_op | source)
XLA Modules:
  0.0 159.9 jit_solution(13817632581752174949)
XLA Ops:
  0.0 1.0 slice.3
  1.0 1.3 collective-permute-start
  2.3 2.3 %collective-permute-done.below = f32[6,8,16,128]{3,2,1,0:T(8,128)S(1)} collective-permute-done((f32[6,8,16,128]{3,2,1,0:T(8,128)S(1)}, f32[6,8,16,128]{3,2,1,0:T(8,128)S(1)}, u32[]{:S(2)}, u32[]{:S(2)}) %collective-permute-start) | collective-permute-done | bytes 393248 | tf_op jit(solution)/shard_map/ppermute | solution.py:496
  4.6 1.9 %copy-done = f32[6,64,16,128]{3,2,1,0:T(8,128)S(1)} copy-done((f32[6,64,16,128]{3,2,1,0:T(8,128)S(1)}, f32[6,64,16,128]{3,2,1,0:T(8,128)}, u32[]{:S(2)}) %copy-start) | copy-done | bytes 3145752
  6.5 1.4 pack_zone.1._
  8.0 7.4 %all-to-all-start = ((f32[8,12,24,128]{3,2,1,0:T(8,128)}), f32[8,12,24,128]{3,2,1,0:T(8,128)S(1)}, u32[]{:S(2)}, u32[]{:S(2)}) async-start(f32[8,12,24,128]{3,2,1,0:T(8,128)} %pack_zone.1._), calls=%async_computation | async-start | bytes 2359296 | tf_op jit(solution)/shard_map/all_to_all | solution.py:501
  15.4 1.3 collective-permute-start.3
  17.4 0.1 pad_add_fusion.place
  17.5 1.9 %copy-done.1 = f32[6,64,16,128]{3,2,1,0:T(8,128)S(1)} copy-done((f32[6,64,16,128]{3,2,1,0:T(8,128)S(1)}, f32[6,64,16,128]{3,2,1,0:T(8,128)}, u32[]{:S(2)}) %copy-start.1) | copy-done | bytes 3145752
  19.4 0.2 first_edges_mid.1
  19.6 2.1 %collective-permute-start.5 = (f32[6,8,8,128]{3,2,1,0:T(8,128)S(1)}, f32[6,8,8,128]{3,2,1,0:T(8,128)S(1)}, u32[]{:S(2)}, u32[]{:S(2)}) collective-permute-start(f32[6,8,8,128]{3,2,1,0:T(8,128)S(1)} %get-tuple-element.52), channel_id=1, source_target_pairs={{0,1},{1,2},{2,3},{3,4},{4,5},{5,6},{6,7},{7,0},{8,9},{9,10},{10,1... | collective-permute-start | bytes 589832 | tf_op jit(solution)/shard_map/ppermute | solution.py:484
  21.6 2.8 %collective-permute-start.6 = (f32[6,8,8,128]{3,2,1,0:T(8,128)S(1)}, f32[6,8,8,128]{3,2,1,0:T(8,128)S(1)}, u32[]{:S(2)}, u32[]{:S(2)}) collective-permute-start(f32[6,8,8,128]{3,2,1,0:T(8,128)S(1)} %get-tuple-element.53), channel_id=1, source_target_pairs={{0,7},{1,0},{2,1},{3,2},{4,3},{5,4},{6,5},{7,6},{8,15},{9,8},{10,9... | collective-permute-start | bytes 589832 | tf_op jit(solution)/shard_map/ppermute | solution.py:484
  24.4 18.9 %all-to-all-done.got = f32[8,12,24,128]{3,2,1,0:T(8,128)S(1)} async-done(((f32[8,12,24,128]{3,2,1,0:T(8,128)}), f32[8,12,24,128]{3,2,1,0:T(8,128)S(1)}, u32[]{:S(2)}, u32[]{:S(2)}) %all-to-all-start) | async-done | bytes 1179680 | tf_op jit(solution)/shard_map/all_to_all | solution.py:501
  43.4 12.7 %step_zone.1 = (f32[8,6,16,128]{3,2,1,0:T(8,128)S(1)}, f32[8,6,16,128]{3,2,1,0:T(8,128)S(1)}, f32[8,128]{1,0:T(8,128)S(1)}) custom-call(s32[2]{0:T(128)S(1)} %pad_add_fusion.place, s32[4,3]{1,0:T(4,128)S(1)} %copy-done.6, f32[6]{0:T(128)S(1)} %copy-done.7, f32[1]{0:T(128)S(6)} %copy.10.swirl, f32[1]{0:T(128)} %collective-permute-done.3.next_swirl, ...), custom_call_target="tpu_custom_call" | custom-call | flops 10000000000 | bytes 10000000 | tf_op jit(solution)/shard_map/step_zone/pallas_call | solution.py:233
  56.1 6.4 %collective-permute-start.4 = (f32[8,6,16,128]{3,2,1,0:T(8,128)S(1)}, f32[8,6,16,128]{3,2,1,0:T(8,128)S(1)}, u32[]{:S(2)}, u32[]{:S(2)}) collective-permute-start(f32[8,6,16,128]{3,2,1,0:T(8,128)S(1)} %get-tuple-element.50), channel_id=1, source_target_pairs={{0,8},{8,16},{16,24},{1,9},{9,17},{17,25},{2,10},{10,18},{18,26},{... | collective-permute-start | bytes 1179656 | tf_op jit(solution)/shard_map/ppermute | solution.py:529
  62.5 3.5 %stage0_mid.1 = (f32[6,32,16,128]{3,2,1,0:T(8,128)S(1)}, f32[6,8,8,128]{3,2,1,0:T(8,128)S(1)}, f32[6,8,8,128]{3,2,1,0:T(8,128)S(1)}, f32[8,128]{1,0:T(8,128)S(1)}) custom-call(f32[6]{0:T(128)S(1)} %copy-done.7, f32[1]{0:T(128)S(6)} %copy.10.swirl, f32[6]{0:T(128)S(1)} %copy-done.8, f32[6,6]{1,0:T(8,128)S(1)} %copy-done.5, f32[6,64,16,128]{3,2,1,0:T(8,128)S(1)} %copy-done.2, ...), custom_call_target="tpu_custom_call" | custom-call | flops 10000000000 | bytes 10000000 | tf_op jit(solution)/shard_map/stage0_mid/pallas_call | solution.py:466
  66.1 0.0 copy-start.9
  66.1 1.1 pad_maximum_fusion
  67.2 0.3 copy-done.9
  67.5 4.3 %all-to-all-start.1 = ((f32[8,12,16,128]{3,2,1,0:T(8,128)}), f32[8,12,16,128]{3,2,1,0:T(8,128)S(1)}, u32[]{:S(2)}, u32[]{:S(2)}) async-start(f32[8,12,16,128]{3,2,1,0:T(8,128)} %pad_maximum_fusion), calls=%async_computation.1 | async-start | bytes 1572864 | tf_op jit(solution)/shard_map/all_to_all | solution.py:534
  71.8 1.9 %copy-done.3 = f32[6,64,16,128]{3,2,1,0:T(8,128)S(1)} copy-done((f32[6,64,16,128]{3,2,1,0:T(8,128)S(1)}, f32[6,64,16,128]{3,2,1,0:T(8,128)}, u32[]{:S(2)}) %copy-start.3) | copy-done | bytes 3145752
  73.7 0.2 first_edges_ends.1
  73.9 2.3 %collective-permute-start.1 = (f32[6,8,8,128]{3,2,1,0:T(8,128)S(1)}, f32[6,8,8,128]{3,2,1,0:T(8,128)S(1)}, u32[]{:S(2)}, u32[]{:S(2)}) collective-permute-start(f32[6,8,8,128]{3,2,1,0:T(8,128)S(1)} %get-tuple-element.48), channel_id=1, source_target_pairs={{0,1},{1,2},{2,3},{3,4},{4,5},{5,6},{6,7},{7,0},{8,9},{9,10},{10,1... | collective-permute-start | bytes 589832 | tf_op jit(solution)/shard_map/ppermute | solution.py:484
  76.1 2.6 %collective-permute-start.2 = (f32[6,8,8,128]{3,2,1,0:T(8,128)S(1)}, f32[6,8,8,128]{3,2,1,0:T(8,128)S(1)}, u32[]{:S(2)}, u32[]{:S(2)}) collective-permute-start(f32[6,8,8,128]{3,2,1,0:T(8,128)S(1)} %get-tuple-element.49), channel_id=1, source_target_pairs={{0,7},{1,0},{2,1},{3,2},{4,3},{5,4},{6,5},{7,6},{8,15},{9,8},{10,9... | collective-permute-start | bytes 589832 | tf_op jit(solution)/shard_map/ppermute | solution.py:484
  78.7 4.7 %collective-permute-start.10 = (f32[6,8,8,128]{3,2,1,0:T(8,128)S(1)}, f32[6,8,8,128]{3,2,1,0:T(8,128)S(1)}, u32[]{:S(2)}, u32[]{:S(2)}) collective-permute-start(f32[6,8,8,128]{3,2,1,0:T(8,128)S(1)} %get-tuple-element.68), channel_id=1, source_target_pairs={{0,7},{1,0},{2,1},{3,2},{4,3},{5,4},{6,5},{7,6},{8,15},{9,8},{10,9... | collective-permute-start | bytes 589832 | tf_op jit(solution)/shard_map/ppermute | solution.py:484
  83.4 10.1 %all-to-all-done.1.got = f32[8,12,16,128]{3,2,1,0:T(8,128)S(1)} async-done(((f32[8,12,16,128]{3,2,1,0:T(8,128)}), f32[8,12,16,128]{3,2,1,0:T(8,128)S(1)}, u32[]{:S(2)}, u32[]{:S(2)}) %all-to-all-start.1) | async-done | bytes 786464 | tf_op jit(solution)/shard_map/all_to_all | solution.py:534
  93.6 0.3 unpack_ghosts.1
  93.8 1.3 collective-permute-done.1.refs_1_
  95.2 0.3 copy-done.4
  95.5 3.5 %stage0_ends.1 = (f32[6,32,16,128]{3,2,1,0:T(8,128)S(1)}, f32[6,8,8,128]{3,2,1,0:T(8,128)S(1)}, f32[6,8,8,128]{3,2,1,0:T(8,128)S(1)}, f32[8,128]{1,0:T(8,128)S(1)}) custom-call(f32[6]{0:T(128)S(1)} %copy-done.7, f32[1]{0:T(128)S(6)} %copy.10.swirl, f32[6]{0:T(128)S(1)} %copy-done.8, f32[6,6]{1,0:T(8,128)S(1)} %copy-done.5, f32[6,64,16,128]{3,2,1,0:T(8,128)S(1)} %copy-done.4, ...), custom_call_target="tpu_custom_call" | custom-call | flops 10000000000 | bytes 10000000 | tf_op jit(solution)/shard_map/stage0_ends/pallas_call | solution.py:466
  99.0 9.4 %collective-permute-start.7 = (f32[6,8,8,128]{3,2,1,0:T(8,128)S(1)}, f32[6,8,8,128]{3,2,1,0:T(8,128)S(1)}, u32[]{:S(2)}, u32[]{:S(2)}) collective-permute-start(f32[6,8,8,128]{3,2,1,0:T(8,128)S(1)} %get-tuple-element.62), channel_id=1, source_target_pairs={{0,1},{1,2},{2,3},{3,4},{4,5},{5,6},{6,7},{7,0},{8,9},{9,10},{10,1... | collective-permute-start | bytes 589832 | tf_op jit(solution)/shard_map/ppermute | solution.py:484
  108.4 3.5 %stage1_mid.1 = (f32[6,32,16,128]{3,2,1,0:T(8,128)S(1)}, f32[6,8,8,128]{3,2,1,0:T(8,128)S(1)}, f32[6,8,8,128]{3,2,1,0:T(8,128)S(1)}, f32[8,128]{1,0:T(8,128)S(1)}) custom-call(f32[6]{0:T(128)S(1)} %copy-done.7, f32[1]{0:T(128)S(6)} %copy.10.swirl, f32[6]{0:T(128)S(1)} %copy-done.8, f32[6,6]{1,0:T(8,128)S(1)} %copy-done.5, f32[6,64,16,128]{3,2,1,0:T(8,128)S(1)} %copy-done.4, ...), custom_call_target="tpu_custom_call" | custom-call | flops 10000000000 | bytes 10000000 | tf_op jit(solution)/shard_map/stage1_mid/pallas_call | solution.py:466
  112.0 2.1 %collective-permute-start.13 = (f32[6,8,8,128]{3,2,1,0:T(8,128)S(1)}, f32[6,8,8,128]{3,2,1,0:T(8,128)S(1)}, u32[]{:S(2)}, u32[]{:S(2)}) collective-permute-start(f32[6,8,8,128]{3,2,1,0:T(8,128)S(1)} %get-tuple-element.76), channel_id=1, source_target_pairs={{0,1},{1,2},{2,3},{3,4},{4,5},{5,6},{6,7},{7,0},{8,9},{9,10},{10,1... | collective-permute-start | bytes 589832 | tf_op jit(solution)/shard_map/ppermute | solution.py:484
  114.0 2.7 %collective-permute-start.14 = (f32[6,8,8,128]{3,2,1,0:T(8,128)S(1)}, f32[6,8,8,128]{3,2,1,0:T(8,128)S(1)}, u32[]{:S(2)}, u32[]{:S(2)}) collective-permute-start(f32[6,8,8,128]{3,2,1,0:T(8,128)S(1)} %get-tuple-element.77), channel_id=1, source_target_pairs={{0,7},{1,0},{2,1},{3,2},{4,3},{5,4},{6,5},{7,6},{8,15},{9,8},{10,9... | collective-permute-start | bytes 589832 | tf_op jit(solution)/shard_map/ppermute | solution.py:484
  116.8 5.3 %collective-permute-done.7.refs_1_ = f32[6,8,8,128]{3,2,1,0:T(8,128)S(1)} collective-permute-done((f32[6,8,8,128]{3,2,1,0:T(8,128)S(1)}, f32[6,8,8,128]{3,2,1,0:T(8,128)S(1)}, u32[]{:S(2)}, u32[]{:S(2)}) %collective-permute-start.7) | collective-permute-done | bytes 196640 | tf_op jit(solution)/shard_map/ppermute | solution.py:484
  122.1 3.6 %stage1_ends.1 = (f32[6,32,16,128]{3,2,1,0:T(8,128)S(1)}, f32[6,8,8,128]{3,2,1,0:T(8,128)S(1)}, f32[6,8,8,128]{3,2,1,0:T(8,128)S(1)}, f32[8,128]{1,0:T(8,128)S(1)}) custom-call(f32[6]{0:T(128)S(1)} %copy-done.7, f32[1]{0:T(128)S(6)} %copy.10.swirl, f32[6]{0:T(128)S(1)} %copy-done.8, f32[6,6]{1,0:T(8,128)S(1)} %copy-done.5, f32[6,64,16,128]{3,2,1,0:T(8,128)S(1)} %copy-done.4, ...), custom_call_target="tpu_custom_call" | custom-call | flops 10000000000 | bytes 10000000 | tf_op jit(solution)/shard_map/stage1_ends/pallas_call | solution.py:466
  125.7 2.5 %collective-permute-start.11 = (f32[6,8,8,128]{3,2,1,0:T(8,128)S(1)}, f32[6,8,8,128]{3,2,1,0:T(8,128)S(1)}, u32[]{:S(2)}, u32[]{:S(2)}) collective-permute-start(f32[6,8,8,128]{3,2,1,0:T(8,128)S(1)} %get-tuple-element.71), channel_id=1, source_target_pairs={{0,1},{1,2},{2,3},{3,4},{4,5},{5,6},{6,7},{7,0},{8,9},{9,10},{10,1... | collective-permute-start | bytes 589832 | tf_op jit(solution)/shard_map/ppermute | solution.py:484
  128.2 2.2 %collective-permute-start.12 = (f32[6,8,8,128]{3,2,1,0:T(8,128)S(1)}, f32[6,8,8,128]{3,2,1,0:T(8,128)S(1)}, u32[]{:S(2)}, u32[]{:S(2)}) collective-permute-start(f32[6,8,8,128]{3,2,1,0:T(8,128)S(1)} %get-tuple-element.72), channel_id=1, source_target_pairs={{0,7},{1,0},{2,1},{3,2},{4,3},{5,4},{6,5},{7,6},{8,15},{9,8},{10,9... | collective-permute-start | bytes 589832 | tf_op jit(solution)/shard_map/ppermute | solution.py:484
  130.5 3.6 %stage2_mid.1 = (f32[6,32,16,128]{3,2,1,0:T(8,128)S(1)}, f32[6,8,8,128]{3,2,1,0:T(8,128)S(1)}, f32[6,8,8,128]{3,2,1,0:T(8,128)S(1)}, f32[8,128]{1,0:T(8,128)S(1)}) custom-call(f32[6]{0:T(128)S(1)} %copy-done.7, f32[1]{0:T(128)S(6)} %copy.10.swirl, f32[6]{0:T(128)S(1)} %copy-done.8, f32[6,6]{1,0:T(8,128)S(1)} %copy-done.5, f32[6,64,16,128]{3,2,1,0:T(8,128)S(1)} %copy-done.4, ...), custom_call_target="tpu_custom_call" | custom-call | flops 10000000000 | bytes 10000000 | tf_op jit(solution)/shard_map/stage2_mid/pallas_call | solution.py:466
  134.0 0.1 collective-permute-start.17
  134.1 4.7 %collective-permute-start.18 = (f32[6,8,8,128]{3,2,1,0:T(8,128)S(1)}, f32[6,8,8,128]{3,2,1,0:T(8,128)S(1)}, u32[]{:S(2)}, u32[]{:S(2)}) collective-permute-start(f32[6,8,8,128]{3,2,1,0:T(8,128)S(1)} %get-tuple-element.86), channel_id=1, source_target_pairs={{0,7},{1,0},{2,1},{3,2},{4,3},{5,4},{6,5},{7,6},{8,15},{9,8},{10,9... | collective-permute-start | bytes 589832 | tf_op jit(solution)/shard_map/ppermute | solution.py:484
  138.8 1.8 %collective-permute-done.11.refs_1_ = f32[6,8,8,128]{3,2,1,0:T(8,128)S(1)} collective-permute-done((f32[6,8,8,128]{3,2,1,0:T(8,128)S(1)}, f32[6,8,8,128]{3,2,1,0:T(8,128)S(1)}, u32[]{:S(2)}, u32[]{:S(2)}) %collective-permute-start.11) | collective-permute-done | bytes 196640 | tf_op jit(solution)/shard_map/ppermute | solution.py:484
  140.5 3.5 %stage2_ends.1 = (f32[6,32,16,128]{3,2,1,0:T(8,128)S(1)}, f32[6,8,8,128]{3,2,1,0:T(8,128)S(1)}, f32[6,8,8,128]{3,2,1,0:T(8,128)S(1)}, f32[8,128]{1,0:T(8,128)S(1)}) custom-call(f32[6]{0:T(128)S(1)} %copy-done.7, f32[1]{0:T(128)S(6)} %copy.10.swirl, f32[6]{0:T(128)S(1)} %copy-done.8, f32[6,6]{1,0:T(8,128)S(1)} %copy-done.5, f32[6,64,16,128]{3,2,1,0:T(8,128)S(1)} %copy-done.4, ...), custom_call_target="tpu_custom_call" | custom-call | flops 10000000000 | bytes 10000000 | tf_op jit(solution)/shard_map/stage2_ends/pallas_call | solution.py:466
  144.1 2.5 %collective-permute-start.15 = (f32[6,8,8,128]{3,2,1,0:T(8,128)S(1)}, f32[6,8,8,128]{3,2,1,0:T(8,128)S(1)}, u32[]{:S(2)}, u32[]{:S(2)}) collective-permute-start(f32[6,8,8,128]{3,2,1,0:T(8,128)S(1)} %get-tuple-element.80), channel_id=1, source_target_pairs={{0,1},{1,2},{2,3},{3,4},{4,5},{5,6},{6,7},{7,0},{8,9},{9,10},{10,1... | collective-permute-start | bytes 589832 | tf_op jit(solution)/shard_map/ppermute | solution.py:484
  146.6 2.2 %collective-permute-start.16 = (f32[6,8,8,128]{3,2,1,0:T(8,128)S(1)}, f32[6,8,8,128]{3,2,1,0:T(8,128)S(1)}, u32[]{:S(2)}, u32[]{:S(2)}) collective-permute-start(f32[6,8,8,128]{3,2,1,0:T(8,128)S(1)} %get-tuple-element.81), channel_id=1, source_target_pairs={{0,7},{1,0},{2,1},{3,2},{4,3},{5,4},{6,5},{7,6},{8,15},{9,8},{10,9... | collective-permute-start | bytes 589832 | tf_op jit(solution)/shard_map/ppermute | solution.py:484
  148.9 4.8 %stage3_mid.1 = (f32[6,64,16,128]{3,2,1,0:T(8,128)}, f32[8,128]{1,0:T(8,128)S(1)}) custom-call(f32[6]{0:T(128)S(1)} %copy-done.7, f32[1]{0:T(128)S(6)} %copy.10.swirl, f32[6]{0:T(128)S(1)} %copy-done.8, f32[6,6]{1,0:T(8,128)S(1)} %copy-done.5, f32[6,64,16,128]{3,2,1,0:T(8,128)S(1)} %copy-done.4, f32[6,8,8,128]{3,2,1,0:T(8,128)S(1)} %collective-permute-done.17.refs_1_, ...), custom_call_target="tpu_custom_call" | custom-call | flops 10000000000 | bytes 10000000 | tf_op jit(solution)/shard_map/stage3_mid/pallas_call | solution.py:466
  153.7 0.8 collective-permute-done.16.refs_2_
  154.4 5.3 %stage3_ends.1 = (f32[6,64,16,128]{3,2,1,0:T(8,128)}, f32[8,128]{1,0:T(8,128)}) custom-call(f32[6]{0:T(128)S(1)} %copy-done.7, f32[1]{0:T(128)S(6)} %copy.10.swirl, f32[6]{0:T(128)S(1)} %copy-done.8, f32[6,6]{1,0:T(8,128)S(1)} %copy-done.5, f32[6,64,16,128]{3,2,1,0:T(8,128)S(1)} %copy-done.4, ...), custom_call_target="tpu_custom_call", output_to_operand_aliasing={{0}: (13, {})} | custom-call | flops 10000000000 | bytes 10000000 | tf_op jit(solution)/shard_map/stage3_ends/pallas_call | solution.py:466
  (35 shorter events, 0.1 us)
Async XLA Ops:
  1.0 3.6 %collective-permute-start = (f32[6,8,16,128]{3,2,1,0:T(8,128)S(1)}, f32[6,8,16,128]{3,2,1,0:T(8,128)S(1)}, u32[]{:S(2)}, u32[]{:S(2)}) collective-permute-start(f32[6,8,16,128]{3,2,1,0:T(8,128)S(1)} %slice.3), channel_id=1, source_target_pairs={{8,0},{16,8},{24,16},{9,1},{17,9},{25,17},{10,2},{18,10},{26,18},{... | collective-permute-start | bytes 1179656 | tf_op jit(solution)/shard_map/ppermute | solution.py:496
  4.6 1.9 %copy-start = (f32[6,64,16,128]{3,2,1,0:T(8,128)S(1)}, f32[6,64,16,128]{3,2,1,0:T(8,128)}, u32[]{:S(2)}) copy-start(f32[6,64,16,128]{3,2,1,0:T(8,128)} %refs_0_.15) | copy-start | bytes 9437188
  8.0 9.4 %copy-start.11 = (f32[16,16,32]{2,1,0:T(8,128)S(1)}, f32[16,16,32]{2,1,0:T(8,128)}, u32[]{:S(2)}) copy-start(f32[16,16,32]{2,1,0:T(8,128)} %param.8) | copy-start | bytes 98308
  8.0 35.3 %all-to-all-start = ((f32[8,12,24,128]{3,2,1,0:T(8,128)}), f32[8,12,24,128]{3,2,1,0:T(8,128)S(1)}, u32[]{:S(2)}, u32[]{:S(2)}) async-start(f32[8,12,24,128]{3,2,1,0:T(8,128)} %pack_zone.1._), calls=%async_computation | async-start | bytes 2359296 | tf_op jit(solution)/shard_map/all_to_all | solution.py:501
  15.4 9.0 %collective-permute-start.3 = (f32[1]{0:T(128)}, f32[1]{0:T(128)}, u32[]{:S(2)}, u32[]{:S(2)}) collective-permute-start(f32[1]{0:T(128)} %param.11), channel_id=1, source_target_pairs={{8,0},{16,8},{24,16},{9,1},{17,9},{25,17},{10,2},{18,10},{26,18},{... | collective-permute-start | bytes 20 | tf_op jit(solution)/shard_map/ppermute | solution.py:497
  17.5 1.9 %copy-start.1 = (f32[6,64,16,128]{3,2,1,0:T(8,128)S(1)}, f32[6,64,16,128]{3,2,1,0:T(8,128)}, u32[]{:S(2)}) copy-start(f32[6,64,16,128]{3,2,1,0:T(8,128)} %refs_0_.15) | copy-start | bytes 9437188
  19.4 24.0 %copy-start.5 = (f32[6,6]{1,0:T(8,128)S(1)}, f32[6,6]{1,0:T(8,128)}, u32[]{:S(2)}) copy-start(f32[6,6]{1,0:T(8,128)} %coupling.17) | copy-start | bytes 436
  19.4 24.0 %copy-start.6 = (s32[4,3]{1,0:T(4,128)S(1)}, s32[4,3]{1,0:T(4,128)}, u32[]{:S(2)}) copy-start(s32[4,3]{1,0:T(4,128)} %offsets.1) | copy-start | bytes 148
  19.4 24.0 %copy-start.7 = (f32[6]{0:T(128)S(1)}, f32[6]{0:T(128)}, u32[]{:S(2)}) copy-start(f32[6]{0:T(128)} %speed.17) | copy-start | bytes 76
  19.4 24.0 %copy-start.8 = (f32[6]{0:T(128)S(1)}, f32[6]{0:T(128)}, u32[]{:S(2)}) copy-start(f32[6]{0:T(128)} %diffusion.17) | copy-start | bytes 76
  19.6 42.9 %collective-permute-start.5 = (f32[6,8,8,128]{3,2,1,0:T(8,128)S(1)}, f32[6,8,8,128]{3,2,1,0:T(8,128)S(1)}, u32[]{:S(2)}, u32[]{:S(2)}) collective-permute-start(f32[6,8,8,128]{3,2,1,0:T(8,128)S(1)} %get-tuple-element.52), channel_id=1, source_target_pairs={{0,1},{1,2},{2,3},{3,4},{4,5},{5,6},{6,7},{7,0},{8,9},{9,10},{10,1... | collective-permute-start | bytes 589832 | tf_op jit(solution)/shard_map/ppermute | solution.py:484
  21.6 40.9 %collective-permute-start.6 = (f32[6,8,8,128]{3,2,1,0:T(8,128)S(1)}, f32[6,8,8,128]{3,2,1,0:T(8,128)S(1)}, u32[]{:S(2)}, u32[]{:S(2)}) collective-permute-start(f32[6,8,8,128]{3,2,1,0:T(8,128)S(1)} %get-tuple-element.53), channel_id=1, source_target_pairs={{0,7},{1,0},{2,1},{3,2},{4,3},{5,4},{6,5},{7,6},{8,15},{9,8},{10,9... | collective-permute-start | bytes 589832 | tf_op jit(solution)/shard_map/ppermute | solution.py:484
  43.4 19.2 %copy-start.2 = (f32[6,64,16,128]{3,2,1,0:T(8,128)S(1)}, f32[6,64,16,128]{3,2,1,0:T(8,128)}, u32[]{:S(2)}) copy-start(f32[6,64,16,128]{3,2,1,0:T(8,128)} %refs_0_.15) | copy-start | bytes 9437188
  56.1 10.0 %collective-permute-start.4 = (f32[8,6,16,128]{3,2,1,0:T(8,128)S(1)}, f32[8,6,16,128]{3,2,1,0:T(8,128)S(1)}, u32[]{:S(2)}, u32[]{:S(2)}) collective-permute-start(f32[8,6,16,128]{3,2,1,0:T(8,128)S(1)} %get-tuple-element.50), channel_id=1, source_target_pairs={{0,8},{8,16},{16,24},{1,9},{9,17},{17,25},{2,10},{10,18},{18,26},{... | collective-permute-start | bytes 1179656 | tf_op jit(solution)/shard_map/ppermute | solution.py:529
  66.1 1.4 copy-start.9
  67.5 26.1 %all-to-all-start.1 = ((f32[8,12,16,128]{3,2,1,0:T(8,128)}), f32[8,12,16,128]{3,2,1,0:T(8,128)S(1)}, u32[]{:S(2)}, u32[]{:S(2)}) async-start(f32[8,12,16,128]{3,2,1,0:T(8,128)} %pad_maximum_fusion), calls=%async_computation.1 | async-start | bytes 1572864 | tf_op jit(solution)/shard_map/all_to_all | solution.py:534
  71.8 1.9 %copy-start.3 = (f32[6,64,16,128]{3,2,1,0:T(8,128)S(1)}, f32[6,64,16,128]{3,2,1,0:T(8,128)}, u32[]{:S(2)}) copy-start(f32[6,64,16,128]{3,2,1,0:T(8,128)} %refs_0_.15) | copy-start | bytes 9437188
  73.9 21.3 %collective-permute-start.1 = (f32[6,8,8,128]{3,2,1,0:T(8,128)S(1)}, f32[6,8,8,128]{3,2,1,0:T(8,128)S(1)}, u32[]{:S(2)}, u32[]{:S(2)}) collective-permute-start(f32[6,8,8,128]{3,2,1,0:T(8,128)S(1)} %get-tuple-element.48), channel_id=1, source_target_pairs={{0,1},{1,2},{2,3},{3,4},{4,5},{5,6},{6,7},{7,0},{8,9},{9,10},{10,1... | collective-permute-start | bytes 589832 | tf_op jit(solution)/shard_map/ppermute | solution.py:484
  76.1 19.0 %collective-permute-start.2 = (f32[6,8,8,128]{3,2,1,0:T(8,128)S(1)}, f32[6,8,8,128]{3,2,1,0:T(8,128)S(1)}, u32[]{:S(2)}, u32[]{:S(2)}) collective-permute-start(f32[6,8,8,128]{3,2,1,0:T(8,128)S(1)} %get-tuple-element.49), channel_id=1, source_target_pairs={{0,7},{1,0},{2,1},{3,2},{4,3},{5,4},{6,5},{7,6},{8,15},{9,8},{10,9... | collective-permute-start | bytes 589832 | tf_op jit(solution)/shard_map/ppermute | solution.py:484
  78.7 29.7 %collective-permute-start.9 = (f32[6,8,8,128]{3,2,1,0:T(8,128)S(1)}, f32[6,8,8,128]{3,2,1,0:T(8,128)S(1)}, u32[]{:S(2)}, u32[]{:S(2)}) collective-permute-start(f32[6,8,8,128]{3,2,1,0:T(8,128)S(1)} %get-tuple-element.67), channel_id=1, source_target_pairs={{0,1},{1,2},{2,3},{3,4},{4,5},{5,6},{6,7},{7,0},{8,9},{9,10},{10,1... | collective-permute-start | bytes 589832 | tf_op jit(solution)/shard_map/ppermute | solution.py:484
  78.7 29.7 %collective-permute-start.10 = (f32[6,8,8,128]{3,2,1,0:T(8,128)S(1)}, f32[6,8,8,128]{3,2,1,0:T(8,128)S(1)}, u32[]{:S(2)}, u32[]{:S(2)}) collective-permute-start(f32[6,8,8,128]{3,2,1,0:T(8,128)S(1)} %get-tuple-element.68), channel_id=1, source_target_pairs={{0,7},{1,0},{2,1},{3,2},{4,3},{5,4},{6,5},{7,6},{8,15},{9,8},{10,9... | collective-permute-start | bytes 589832 | tf_op jit(solution)/shard_map/ppermute | solution.py:484
  93.6 1.9 %copy-start.4 = (f32[6,64,16,128]{3,2,1,0:T(8,128)S(1)}, f32[6,64,16,128]{3,2,1,0:T(8,128)}, u32[]{:S(2)}) copy-start(f32[6,64,16,128]{3,2,1,0:T(8,128)} %refs_0_.15) | copy-start | bytes 9437188
  95.5 13.0 %copy-start.10 = (f32[6,32,16,128]{3,2,1,0:T(8,128)S(1)}, f32[6,32,16,128]{3,2,1,0:T(8,128)}, u32[]{:S(2)}) copy-start(f32[6,32,16,128]{3,2,1,0:T(8,128)} %copy-done.9) | copy-start | bytes 4718596
  99.0 23.1 %collective-permute-start.7 = (f32[6,8,8,128]{3,2,1,0:T(8,128)S(1)}, f32[6,8,8,128]{3,2,1,0:T(8,128)S(1)}, u32[]{:S(2)}, u32[]{:S(2)}) collective-permute-start(f32[6,8,8,128]{3,2,1,0:T(8,128)S(1)} %get-tuple-element.62), channel_id=1, source_target_pairs={{0,1},{1,2},{2,3},{3,4},{4,5},{5,6},{6,7},{7,0},{8,9},{9,10},{10,1... | collective-permute-start | bytes 589832 | tf_op jit(solution)/shard_map/ppermute | solution.py:484
  108.4 13.7 %collective-permute-start.8 = (f32[6,8,8,128]{3,2,1,0:T(8,128)S(1)}, f32[6,8,8,128]{3,2,1,0:T(8,128)S(1)}, u32[]{:S(2)}, u32[]{:S(2)}) collective-permute-start(f32[6,8,8,128]{3,2,1,0:T(8,128)S(1)} %get-tuple-element.63), channel_id=1, source_target_pairs={{0,7},{1,0},{2,1},{3,2},{4,3},{5,4},{6,5},{7,6},{8,15},{9,8},{10,9... | collective-permute-start | bytes 589832 | tf_op jit(solution)/shard_map/ppermute | solution.py:484
  112.0 18.5 %collective-permute-start.13 = (f32[6,8,8,128]{3,2,1,0:T(8,128)S(1)}, f32[6,8,8,128]{3,2,1,0:T(8,128)S(1)}, u32[]{:S(2)}, u32[]{:S(2)}) collective-permute-start(f32[6,8,8,128]{3,2,1,0:T(8,128)S(1)} %get-tuple-element.76), channel_id=1, source_target_pairs={{0,1},{1,2},{2,3},{3,4},{4,5},{5,6},{6,7},{7,0},{8,9},{9,10},{10,1... | collective-permute-start | bytes 589832 | tf_op jit(solution)/shard_map/ppermute | solution.py:484
  114.0 16.4 %collective-permute-start.14 = (f32[6,8,8,128]{3,2,1,0:T(8,128)S(1)}, f32[6,8,8,128]{3,2,1,0:T(8,128)S(1)}, u32[]{:S(2)}, u32[]{:S(2)}) collective-permute-start(f32[6,8,8,128]{3,2,1,0:T(8,128)S(1)} %get-tuple-element.77), channel_id=1, source_target_pairs={{0,7},{1,0},{2,1},{3,2},{4,3},{5,4},{6,5},{7,6},{8,15},{9,8},{10,9... | collective-permute-start | bytes 589832 | tf_op jit(solution)/shard_map/ppermute | solution.py:484
  125.7 14.9 %collective-permute-start.11 = (f32[6,8,8,128]{3,2,1,0:T(8,128)S(1)}, f32[6,8,8,128]{3,2,1,0:T(8,128)S(1)}, u32[]{:S(2)}, u32[]{:S(2)}) collective-permute-start(f32[6,8,8,128]{3,2,1,0:T(8,128)S(1)} %get-tuple-element.71), channel_id=1, source_target_pairs={{0,1},{1,2},{2,3},{3,4},{4,5},{5,6},{6,7},{7,0},{8,9},{9,10},{10,1... | collective-permute-start | bytes 589832 | tf_op jit(solution)/shard_map/ppermute | solution.py:484
  128.2 12.3 %collective-permute-start.12 = (f32[6,8,8,128]{3,2,1,0:T(8,128)S(1)}, f32[6,8,8,128]{3,2,1,0:T(8,128)S(1)}, u32[]{:S(2)}, u32[]{:S(2)}) collective-permute-start(f32[6,8,8,128]{3,2,1,0:T(8,128)S(1)} %get-tuple-element.72), channel_id=1, source_target_pairs={{0,7},{1,0},{2,1},{3,2},{4,3},{5,4},{6,5},{7,6},{8,15},{9,8},{10,9... | collective-permute-start | bytes 589832 | tf_op jit(solution)/shard_map/ppermute | solution.py:484
  134.0 14.9 %collective-permute-start.17 = (f32[6,8,8,128]{3,2,1,0:T(8,128)S(1)}, f32[6,8,8,128]{3,2,1,0:T(8,128)S(1)}, u32[]{:S(2)}, u32[]{:S(2)}) collective-permute-start(f32[6,8,8,128]{3,2,1,0:T(8,128)S(1)} %get-tuple-element.85), channel_id=1, source_target_pairs={{0,1},{1,2},{2,3},{3,4},{4,5},{5,6},{6,7},{7,0},{8,9},{9,10},{10,1... | collective-permute-start | bytes 589832 | tf_op jit(solution)/shard_map/ppermute | solution.py:484
  134.1 14.8 %collective-permute-start.18 = (f32[6,8,8,128]{3,2,1,0:T(8,128)S(1)}, f32[6,8,8,128]{3,2,1,0:T(8,128)S(1)}, u32[]{:S(2)}, u32[]{:S(2)}) collective-permute-start(f32[6,8,8,128]{3,2,1,0:T(8,128)S(1)} %get-tuple-element.86), channel_id=1, source_target_pairs={{0,7},{1,0},{2,1},{3,2},{4,3},{5,4},{6,5},{7,6},{8,15},{9,8},{10,9... | collective-permute-start | bytes 589832 | tf_op jit(solution)/shard_map/ppermute | solution.py:484
  144.1 9.5 %collective-permute-start.15 = (f32[6,8,8,128]{3,2,1,0:T(8,128)S(1)}, f32[6,8,8,128]{3,2,1,0:T(8,128)S(1)}, u32[]{:S(2)}, u32[]{:S(2)}) collective-permute-start(f32[6,8,8,128]{3,2,1,0:T(8,128)S(1)} %get-tuple-element.80), channel_id=1, source_target_pairs={{0,1},{1,2},{2,3},{3,4},{4,5},{5,6},{6,7},{7,0},{8,9},{9,10},{10,1... | collective-permute-start | bytes 589832 | tf_op jit(solution)/shard_map/ppermute | solution.py:484
  146.6 7.8 %collective-permute-start.16 = (f32[6,8,8,128]{3,2,1,0:T(8,128)S(1)}, f32[6,8,8,128]{3,2,1,0:T(8,128)S(1)}, u32[]{:S(2)}, u32[]{:S(2)}) collective-permute-start(f32[6,8,8,128]{3,2,1,0:T(8,128)S(1)} %get-tuple-element.81), channel_id=1, source_target_pairs={{0,7},{1,0},{2,1},{3,2},{4,3},{5,4},{6,5},{7,6},{8,15},{9,8},{10,9... | collective-permute-start | bytes 589832 | tf_op jit(solution)/shard_map/ppermute | solution.py:484
